TPU v7x, 512 devices: a whole 4x8x8 slice. The times are simulated.
512 devices in a mesh: row: 32 (over x, z), col: 16 (over y, core).
Axes of the slice: x: 4, y: 8, z: 8, core: 2. Of those that a mesh axis runs over, the one named last changes fastest.
Arguments:
- node_coords: int32 [3, 65536], P(None, ('row', 'col')), may hold values from 0 to 1023
- inv_range: float32 [3], replicated, may hold values from 0.008 to 0.03
- mode_block: float32 [96, 65536], P(None, ('row', 'col')), may hold values from -40 to 40
Outputs:
- basis: float32 [96, 65536], P(None, ('row', 'col'))
- ritz: float32 [96, 96], replicated
All inputs are finite; a program needn't handle non-finite values.
Results may differ from a plain program's by a relative error of at most 0.00055.
The roundings to bfloat16 on the way count: a program that leaves them out, or rounds other values in their place, can miss the bound.
Values may be sent and summed in bfloat16 or wider, within the bound.
No kernel may reach another device: no remote copies, remote signals or barrier semaphores. Data moves between devices by JAX's collectives and lax.ppermute only.
A program may use at most 64 MiB of HBM per device.

v0:
```python
import math

import jax
import jax.numpy as jnp
from jax import lax
from jax.sharding import PartitionSpec as P

NUGGET = 0.25


def covariance(row_parts, col_parts, inv_range):
    diff = row_parts - col_parts
    delta_x = diff[0].astype(jnp.float32) * inv_range[0]
    delta_y = diff[1].astype(jnp.float32) * inv_range[1]
    delta_z = diff[2].astype(jnp.float32) * inv_range[2]
    squared = delta_x * delta_x + delta_y * delta_y + delta_z * delta_z
    return jnp.exp(1.0 - jnp.sqrt(1.0 + squared)).astype(jnp.bfloat16)


def body(node_coords, inv_range, mode_block):
    mode_count = mode_block.shape[0]
    node_dev = mode_block.shape[1]
    row_count = lax.axis_size("row")
    col_count = lax.axis_size("col")
    node_total = node_dev * row_count * col_count
    low_modes = mode_block.astype(jnp.bfloat16)
    stripe_len = node_dev * col_count
    mode_gram = lax.psum(
        jnp.dot(mode_block, mode_block.T, precision=lax.Precision.HIGHEST), ("row", "col")
    )
    stripe_pts = lax.all_gather(node_coords, "col", axis=1, tiled=True)
    start_rows = jnp.zeros((mode_count, stripe_len), jnp.float32)
    piece_low = lax.all_gather(low_modes, "row", axis=1, tiled=True)
    piece_pts = lax.all_gather(node_coords, "row", axis=1, tiled=True)
    shards = piece_low.shape[1] // node_dev
    group_size = math.gcd(shards, 4)
    block_count = shards // group_size
    low_blocks = piece_low.reshape(mode_count, block_count, group_size * node_dev).transpose(
        1, 0, 2
    )
    pts_blocks = piece_pts.reshape(3, block_count, group_size * node_dev).transpose(1, 0, 2)

    def one_block(partial_rows, blocks_in):
        block_low, block_pts = blocks_in
        kernel = covariance(stripe_pts[:, :, None], block_pts[:, None, :], inv_range)
        update = lax.dot_general(
            block_low, kernel, (((1,), (1,)), ((), ())), preferred_element_type=jnp.float32
        )
        return (partial_rows + update, None)

    finished, _ = lax.scan(one_block, start_rows, (low_blocks, pts_blocks))
    power_image = lax.psum_scatter(finished, "col", scatter_dimension=1, tiled=True)
    power_image = power_image + NUGGET * mode_block
    local_image = jnp.dot(power_image, power_image.T, precision=lax.Precision.HIGHEST)
    local_cross = jnp.dot(mode_block, power_image.T, precision=lax.Precision.HIGHEST)
    image_gram, cross = lax.psum((local_image, local_cross), ("row", "col"))
    image_gram = image_gram / node_total
    mode_gram = mode_gram / node_total
    cross = cross / node_total
    lower = jnp.linalg.cholesky(image_gram)
    basis = jax.scipy.linalg.solve_triangular(lower, power_image, lower=True)
    lower_modes = jnp.linalg.cholesky(mode_gram)
    half_solved = jax.scipy.linalg.solve_triangular(lower_modes, cross, lower=True)
    ritz = jax.scipy.linalg.solve_triangular(lower_modes, half_solved.T, lower=True).T
    return (basis, ritz)


def solution(mesh):
    placed = (P(None, ("row", "col")), P(), P(None, ("row", "col")))
    return jax.shard_map(
        body, mesh=mesh, in_specs=placed, out_specs=(P(None, ("row", "col")), P()), check_vma=False
    )
```

profile of v0, /device:TPU:1, one launch (start us, length us, event | category | flops | bytes accessed | tf_op | source)
XLA Modules:
  0.0 616.7 jit_solution(14391900313729339050)
XLA Ops:
  7.2 43.4 %all_gather.11 = s32[3,4096]{1,0:T(4,128)S(1)} all-gather(s32[3,128]{1,0:T(4,128)} %param.8), channel_id=1, replica_groups=mesh['row'=32,'col'=16] {'row'}, dimensions={1}, use_global_device_ids=true | all-gather | bytes 50688 | tf_op jit(solution)/shard_map/all_gather | solution.py:34
  50.6 30.7 %all_gather.10 = s32[3,2048]{1,0:T(4,128)S(1)} all-gather(s32[3,128]{1,0:T(4,128)} %param.8), channel_id=1, replica_groups=mesh['row'=32,'col'=16] {'col'}, dimensions={1}, use_global_device_ids=true | all-gather | bytes 26112 | tf_op jit(solution)/shard_map/all_gather | solution.py:31
  82.1 38.2 %all_gather.9 = bf16[96,4096]{1,0:T(8,128)(2,1)S(1)} all-gather(bf16[96,128]{1,0:T(8,128)(2,1)S(1)} %convert_element_type.21), channel_id=1, replica_groups=mesh['row'=32,'col'=16] {'row'}, dimensions={1}, use_global_device_ids=true | all-gather | bytes 811008 | tf_op jit(solution)/shard_map/all_gather | solution.py:33
  120.9 111.9 %while.11 = (s32[]{:T(128)}, f32[96,2048]{1,0:T(8,128)S(1)}, bf16[8,96,512]{2,1,0:T(8,128)(2,1)S(1)}, s32[3,2048]{1,0:T(4,128)S(1)}, s32[8,3,512]{2,1,0:T(4,128)S(1)}, /*index=5*/f32[3]{0:T(128)}, s32[]{:T(128)}, s32[]{:T(128)}) while((s32[]{:T(128)}, f32[96,2048]{1,0:T(8,128)S(1)}, bf16[8,96,512]{2,1,0:T(8,128)(2,1)S(1)}, ...), condition=%wide.region_1.2_spmd.clone, body=%wide.region_0.0_spmd.clone.sunk | while | flops 219545600 | bytes 26880216 | solution.py:51
  120.9 4.9 broadcast_subtract_fusion.2
  126.5 8.3 %convolution_add_fusion.2 = f32[96,2048]{1,0:T(8,128)S(1)} fusion(s32[3,2048,512]{2,1,0:T(8,128)} %broadcast_subtract_fusion.2, f32[]{:T(128)} %bitcast.59, f32[]{:T(128)} %bitcast.60, f32[]{:T(128)} %bitcast.61, f32[96,2048]{1,0:T(8,128)S(1)} %get-tuple-element.140, pred[]{:T(512)S(6)} %compare.15, bf16[8,96,512]{2,1,0:T(8,128)(2,1)S(1)} %get-tuple-element.149, ...), kind=kOutput, calls=%fused_computation.17.clone.1 | convolution fusion | flops 216399872 | bytes 14254097 | tf_op jit(solution)/shard_map/while/body/eval_jaxpr/dot_general | solution.py:46
  134.9 4.9 broadcast_subtract_fusion.2
  140.5 8.4 %convolution_add_fusion.2 = f32[96,2048]{1,0:T(8,128)S(1)} fusion(s32[3,2048,512]{2,1,0:T(8,128)} %broadcast_subtract_fusion.2, f32[]{:T(128)} %bitcast.59, f32[]{:T(128)} %bitcast.60, f32[]{:T(128)} %bitcast.61, f32[96,2048]{1,0:T(8,128)S(1)} %get-tuple-element.140, pred[]{:T(512)S(6)} %compare.15, bf16[8,96,512]{2,1,0:T(8,128)(2,1)S(1)} %get-tuple-element.149, ...), kind=kOutput, calls=%fused_computation.17.clone.1 | convolution fusion | flops 216399872 | bytes 14254097 | tf_op jit(solution)/shard_map/while/body/eval_jaxpr/dot_general | solution.py:46
  148.9 4.9 broadcast_subtract_fusion.2
  154.5 8.3 %convolution_add_fusion.2 = f32[96,2048]{1,0:T(8,128)S(1)} fusion(s32[3,2048,512]{2,1,0:T(8,128)} %broadcast_subtract_fusion.2, f32[]{:T(128)} %bitcast.59, f32[]{:T(128)} %bitcast.60, f32[]{:T(128)} %bitcast.61, f32[96,2048]{1,0:T(8,128)S(1)} %get-tuple-element.140, pred[]{:T(512)S(6)} %compare.15, bf16[8,96,512]{2,1,0:T(8,128)(2,1)S(1)} %get-tuple-element.149, ...), kind=kOutput, calls=%fused_computation.17.clone.1 | convolution fusion | flops 216399872 | bytes 14254097 | tf_op jit(solution)/shard_map/while/body/eval_jaxpr/dot_general | solution.py:46
  162.9 4.9 broadcast_subtract_fusion.2
  168.5 8.3 %convolution_add_fusion.2 = f32[96,2048]{1,0:T(8,128)S(1)} fusion(s32[3,2048,512]{2,1,0:T(8,128)} %broadcast_subtract_fusion.2, f32[]{:T(128)} %bitcast.59, f32[]{:T(128)} %bitcast.60, f32[]{:T(128)} %bitcast.61, f32[96,2048]{1,0:T(8,128)S(1)} %get-tuple-element.140, pred[]{:T(512)S(6)} %compare.15, bf16[8,96,512]{2,1,0:T(8,128)(2,1)S(1)} %get-tuple-element.149, ...), kind=kOutput, calls=%fused_computation.17.clone.1 | convolution fusion | flops 216399872 | bytes 14254097 | tf_op jit(solution)/shard_map/while/body/eval_jaxpr/dot_general | solution.py:46
  176.9 4.9 broadcast_subtract_fusion.2
  182.4 8.3 %convolution_add_fusion.2 = f32[96,2048]{1,0:T(8,128)S(1)} fusion(s32[3,2048,512]{2,1,0:T(8,128)} %broadcast_subtract_fusion.2, f32[]{:T(128)} %bitcast.59, f32[]{:T(128)} %bitcast.60, f32[]{:T(128)} %bitcast.61, f32[96,2048]{1,0:T(8,128)S(1)} %get-tuple-element.140, pred[]{:T(512)S(6)} %compare.15, bf16[8,96,512]{2,1,0:T(8,128)(2,1)S(1)} %get-tuple-element.149, ...), kind=kOutput, calls=%fused_computation.17.clone.1 | convolution fusion | flops 216399872 | bytes 14254097 | tf_op jit(solution)/shard_map/while/body/eval_jaxpr/dot_general | solution.py:46
  190.8 4.9 broadcast_subtract_fusion.2
  196.4 8.3 %convolution_add_fusion.2 = f32[96,2048]{1,0:T(8,128)S(1)} fusion(s32[3,2048,512]{2,1,0:T(8,128)} %broadcast_subtract_fusion.2, f32[]{:T(128)} %bitcast.59, f32[]{:T(128)} %bitcast.60, f32[]{:T(128)} %bitcast.61, f32[96,2048]{1,0:T(8,128)S(1)} %get-tuple-element.140, pred[]{:T(512)S(6)} %compare.15, bf16[8,96,512]{2,1,0:T(8,128)(2,1)S(1)} %get-tuple-element.149, ...), kind=kOutput, calls=%fused_computation.17.clone.1 | convolution fusion | flops 216399872 | bytes 14254097 | tf_op jit(solution)/shard_map/while/body/eval_jaxpr/dot_general | solution.py:46
  204.8 4.9 broadcast_subtract_fusion.2
  210.4 8.3 %convolution_add_fusion.2 = f32[96,2048]{1,0:T(8,128)S(1)} fusion(s32[3,2048,512]{2,1,0:T(8,128)} %broadcast_subtract_fusion.2, f32[]{:T(128)} %bitcast.59, f32[]{:T(128)} %bitcast.60, f32[]{:T(128)} %bitcast.61, f32[96,2048]{1,0:T(8,128)S(1)} %get-tuple-element.140, pred[]{:T(512)S(6)} %compare.15, bf16[8,96,512]{2,1,0:T(8,128)(2,1)S(1)} %get-tuple-element.149, ...), kind=kOutput, calls=%fused_computation.17.clone.1 | convolution fusion | flops 216399872 | bytes 14254097 | tf_op jit(solution)/shard_map/while/body/eval_jaxpr/dot_general | solution.py:46
  218.8 4.9 broadcast_subtract_fusion.2
  224.4 8.3 %convolution_add_fusion.2 = f32[96,2048]{1,0:T(8,128)S(1)} fusion(s32[3,2048,512]{2,1,0:T(8,128)} %broadcast_subtract_fusion.2, f32[]{:T(128)} %bitcast.59, f32[]{:T(128)} %bitcast.60, f32[]{:T(128)} %bitcast.61, f32[96,2048]{1,0:T(8,128)S(1)} %get-tuple-element.140, pred[]{:T(512)S(6)} %compare.15, bf16[8,96,512]{2,1,0:T(8,128)(2,1)S(1)} %get-tuple-element.149, ...), kind=kOutput, calls=%fused_computation.17.clone.1 | convolution fusion | flops 216399872 | bytes 14254097 | tf_op jit(solution)/shard_map/while/body/eval_jaxpr/dot_general | solution.py:46
  232.8 0.9 copy-done.1
  233.7 0.8 fusion.35
  234.6 61.7 %reduce-scatter.2.cloned.1.call-done = f32[96,128]{1,0:T(8,128)} async-done(((f32[96,2048]{1,0:T(8,128)}), f32[96,128]{1,0:T(8,128)}) %reduce-scatter.2.cloned.1.call-update) | async-done | bytes 49168 | tf_op jit(solution)/shard_map/reduce_scatter | solution.py:52
  296.3 1.6 convolution_bitcast_fusion.2
  297.9 1.7 fusion.29
  299.6 268.9 %all-reduce.3.cloned.1.call-done = (f32[96,96]{0,1:T(8,128)}, f32[96,96]{0,1:T(8,128)}, f32[96,96]{0,1:T(8,128)}) async-done(((f32[96,96]{0,1:T(8,128)}, f32[96,96]{0,1:T(8,128)}, f32[96,96]{0,1:T(8,128)}), (f32[96,96]{0,1:T(8,128)}, f32[96,96]{0,1:T(8,128)}, f32[96,96]{0,1:T(8,128)})) %all-reduce.3.cloned.1.call-update) | async-done | bytes 110608 | tf_op jit(solution)/shard_map/psum | solution.py:56
  571.2 8.8 %cholesky.55 = f32[96,96]{1,0:T(8,128)S(1)} custom-call(f32[96,96]{1,0:T(8,128)S(1)} %get-tuple-element.86), custom_call_target="Cholesky" | custom-call | tf_op jit(solution)/shard_map/jit(cholesky)/cholesky | solution.py:62
  581.3 7.4 %custom-call.13 = f32[1,96,96]{1,2,0:T(8,128)S(1)} custom-call(f32[1,96,96]{2,1,0:T(8,128)S(1)} %fusion.20), custom_call_target="InvertDiagBlocksLowerTriangular" | custom-call | tf_op jit(solution)/shard_map/jit(_solve_triangular)/triangular_solve | solution.py:64
  588.7 1.1 convolution_bitcast_fusion.1
  590.7 8.8 %cholesky.44 = f32[96,96]{1,0:T(8,128)S(1)} custom-call(f32[96,96]{1,0:T(8,128)S(1)} %get-tuple-element.87), custom_call_target="Cholesky" | custom-call | tf_op jit(solution)/shard_map/jit(cholesky)/cholesky | solution.py:60
  600.8 7.4 %custom-call.9 = f32[1,96,96]{1,2,0:T(8,128)S(1)} custom-call(f32[1,96,96]{2,1,0:T(8,128)S(1)} %fusion.19), custom_call_target="InvertDiagBlocksLowerTriangular" | custom-call | tf_op jit(solution)/shard_map/jit(_solve_triangular)/triangular_solve | solution.py:61
  608.2 1.7 fusion.24
  (56 shorter events, 13.0 us)
Async XLA Ops:
  7.2 289.1 %reduce-scatter.2.cloned.1.call-start = ((), (), s32[]{:S(2)}) async-start(), calls=%async_computation.1 | async-start | bytes 835584 | tf_op jit(solution)/shard_map/reduce_scatter | solution.py:52
  120.8 112.9 %copy-start = (f32[96,128]{1,0:T(8,128)S(1)}, f32[96,128]{1,0:T(8,128)}, u32[]{:S(2)}) copy-start(f32[96,128]{1,0:T(8,128)} %param.10) | copy-start | bytes 147460
  120.9 4.9 copy-start.2
  134.9 4.9 copy-start.2
  148.9 4.9 copy-start.2
  162.9 4.9 copy-start.2
  176.8 4.9 copy-start.2
  190.8 4.9 copy-start.2
  204.8 4.9 copy-start.2
  218.8 4.9 copy-start.2
  232.8 0.9 copy-start.1
  233.7 334.9 %all-reduce.3.cloned.1.call-start = ((), (), s32[]{:S(2)}) async-start(), calls=%async_computation.2 | async-start | bytes 294912 | tf_op jit(solution)/shard_map/psum | solution.py:56
Sparse Core Ops, SparseCore 0:
  233.8 62.4 reduce-scatter.1
  303.3 265.2 all-reduce.2
where the time goes:
time: 618 us; the launch traced here: 617 us
  waiting for transfers between devices  331 us (54%)
  blocking collectives  112 us (18%)
  other arithmetic  77.7 us (13%)
  matrix products  74 us (12%)
  between operations  14.2 us (2%)
  local copies, waits for them, and re-layouts  7.58 us (1%)
    psum x1, waiting for transfers between devices, body(): image_gram, cross = lax.psum((local_image, local_cross), ('row', 'col'))  269 us
    dot_general x8, matrix products, one_block(): lax.dot_general(block_low, kernel, (((1,), (1,)), ((), ())), preferred_el...  66.8 us
    reduce_scatter x1, waiting for transfers between devices, body(): lax.psum_scatter(finished, 'col', scatter_dimension=1, tiled=True)  61.7 us
    all_gather x1, blocking collectives, body(): piece_pts = lax.all_gather(node_coords, 'row', axis=1, tiled=True)  43.4 us
    sub x8, other arithmetic, covariance(): diff = row_parts - col_parts  39.5 us
    all_gather x1, blocking collectives, body(): piece_low = lax.all_gather(low_modes, 'row', axis=1, tiled=True)  38.2 us
    all_gather x1, blocking collectives, body(): stripe_pts = lax.all_gather(node_coords, 'col', axis=1, tiled=True)  30.7 us
  transfers between devices with their start and end apart: 2, of which 2 were waited for; matrix products, arithmetic and copies ran while one was open for 0% of the time, Pallas kernels for 0%

commit v1 on v0

v1 whole, which is shorter than its diff:
```python
import functools
import math

import jax
import jax.numpy as jnp
from jax import lax
from jax.experimental import pallas as pl
from jax.experimental.pallas import tpu as pltpu
from jax.sharding import Mesh, PartitionSpec as P

NUGGET = 0.25
LOG2E = math.log2(math.e)
CENTRE = 512.0
HIGHEST = lax.Precision.HIGHEST
PARAMS = pltpu.CompilerParams(vmem_limit_bytes=48 * 1024 * 1024)


def scaled_coords(pack, scale):
    parts = pack.astype(jnp.float32)
    return (parts[0:8] * 4.0 + (parts[8:16] - CENTRE)) * scale


def scale_rows(range_ref):
    index = lax.broadcasted_iota(jnp.int32, (8, 128), 0)
    picked = jnp.where(
        index == 0,
        range_ref[0],
        jnp.where(index == 1, range_ref[1], jnp.where(index == 2, range_ref[2], 0.0)),
    )
    return picked * LOG2E


def cov_kernel(first, modes, range_ref, row_ref, col_ref, *refs):
    if first:
        out_ref, rows, cols = refs
    else:
        start_ref, out_ref, rows, cols = refs
    pieces, _, width = col_ref.shape
    dests = row_ref.shape[0]
    scale = scale_rows(range_ref)
    for y in range(dests):
        rows[:, y * width : (y + 1) * width] = scaled_coords(row_ref[y], scale)
    if first:
        out_ref[...] = jnp.zeros_like(out_ref)
    else:
        out_ref[...] = start_ref[...]

    @pl.loop(0, pieces // 2)
    def _(step):
        low = []
        for half in range(2):
            piece = step * 2 + half
            low.append(col_ref[piece, 0:modes, :])
            coords = scaled_coords(col_ref[piece, modes : modes + 16, :], scale)
            cols[half * width : (half + 1) * width, :] = coords.T
        low = jnp.concatenate(low, axis=1)
        for pair in range(dests // 2):
            total = LOG2E * LOG2E
            for d in range(3):
                delta = cols[:, d : d + 1] - rows[d : d + 1, pair * 2 * width : (pair + 1) * 2 * width]
                total = total + delta * delta
            cov = jnp.exp2(LOG2E - total * lax.rsqrt(total)).astype(jnp.bfloat16)
            update = jnp.dot(low, cov, preferred_element_type=jnp.float32)
            out_ref[2 * pair] += update[:, :width]
            out_ref[2 * pair + 1] += update[:, width:]


def covariance_part(inv_range, row_pack, col_pack, start=None):
    dests, _, width = row_pack.shape
    modes = col_pack.shape[1] - 16
    pairs = col_pack.shape[0] * dests * width * width
    vmem = pl.BlockSpec(memory_space=pltpu.VMEM)
    args = (inv_range, row_pack, col_pack) + (() if start is None else (start,))
    return pl.pallas_call(
        functools.partial(cov_kernel, start is None, modes),
        out_shape=jax.ShapeDtypeStruct((dests, modes, width), jnp.float32),
        in_specs=[pl.BlockSpec(memory_space=pltpu.SMEM)] + [vmem] * (len(args) - 1),
        out_specs=vmem,
        scratch_shapes=[
            pltpu.VMEM((8, dests * width), jnp.float32),
            pltpu.VMEM((2 * width, 8), jnp.float32),
        ],
        compiler_params=PARAMS,
        cost_estimate=pl.CostEstimate(
            flops=pairs * (2 * modes + 12), bytes_accessed=4 * dests * modes * width, transcendentals=2 * pairs
        ),
    )(*args)


def nt_dot(left, right):
    return lax.dot_general(
        left, right, (((1,), (1,)), ((), ())), precision=HIGHEST, preferred_element_type=jnp.float32
    )


def gram_kernel(part_ref, mode_ref, image_ref, gram_ref):
    image = part_ref[0]
    for y in range(1, part_ref.shape[0]):
        image = image + part_ref[y]
    mode = mode_ref[...]
    image = image + NUGGET * mode
    image_ref[...] = image
    modes = image.shape[0]
    tiles = modes // 8
    slots = gram_ref.shape[0]
    grams = (nt_dot(image, image), nt_dot(mode, image), nt_dot(mode, mode))
    gram_ref[...] = jnp.zeros_like(gram_ref)
    for which, gram in enumerate(grams):
        for t in range(tiles):
            place = which * tiles + t
            slot, level = place % slots, place // slots
            gram_ref[slot, level * 8 : level * 8 + 8, 0:modes] = gram[t * 8 : t * 8 + 8, :]


def spread_kernel(part_ref, out_ref):
    total = part_ref[0]
    for k in range(1, part_ref.shape[0]):
        total = total + part_ref[k]
    for k in range(out_ref.shape[0]):
        out_ref[k] = total


def final_kernel(node_total, gram_ref, image_ref, basis_ref, ritz_ref):
    modes, width = image_ref.shape
    tiles = modes // 8
    slots = gram_ref.shape[0]

    def tile(which, t):
        place = which * tiles + t
        slot, level = place % slots, place // slots
        return gram_ref[slot, level * 8 : level * 8 + 8, :] * (1.0 / node_total)

    lane = lax.broadcasted_iota(jnp.int32, (8, width), 1)
    row = lax.broadcasted_iota(jnp.int32, (8, width), 0)
    left = [[tile(0, t) for t in range(tiles)], [tile(2, t) for t in range(tiles)]]
    right = [
        [image_ref[t * 8 : t * 8 + 8, :] for t in range(tiles)],
        [jnp.where(lane == row + 8 * t, 1.0, 0.0) for t in range(tiles)],
    ]
    for k in range(modes):
        home, sub = divmod(k, 8)
        for m in range(2):
            a, b = left[m], right[m]
            spread = {t: jnp.broadcast_to(a[t][:, k : k + 1], (8, width)) for t in range(home, tiles)}
            inverse = 1.0 / spread[home][sub : sub + 1, :]
            row_a = jnp.broadcast_to(a[home][sub : sub + 1, :] * inverse, (8, width))
            row_b = jnp.broadcast_to(b[home][sub : sub + 1, :] * inverse, (8, width))
            for t in range(home, tiles):
                factor = spread[t]
                if t == home:
                    if sub == 7:
                        continue
                    factor = jnp.where(row > sub, factor, 0.0)
                a[t] = a[t] - factor * row_a
                b[t] = b[t] - factor * row_b

    def finish(m):
        rows = []
        for t in range(tiles):
            pivot = jnp.sum(jnp.where(lane == row + 8 * t, left[m][t], 0.0), axis=1, keepdims=True)
            rows.append(right[m][t] * (1.0 / jnp.sqrt(pivot)))
        return jnp.concatenate(rows, axis=0)

    basis_ref[...] = finish(0)
    inverse = finish(1)[:, 0:modes]
    cross = jnp.concatenate([tile(1, t) for t in range(tiles)], axis=0)[:, 0:modes]
    half = jnp.dot(inverse, cross, precision=HIGHEST, preferred_element_type=jnp.float32)
    ritz_ref[...] = nt_dot(half, inverse)


def call(kernel, out_shape, *args):
    return pl.pallas_call(kernel, out_shape=out_shape, compiler_params=PARAMS)(*args)


def body(node_coords, inv_range, mode_block):
    modes, width = mode_block.shape
    groups, stripes, cores = lax.axis_size("row"), lax.axis_size("y"), lax.axis_size("c")
    node_total = groups * stripes * cores * width
    low = mode_block.astype(jnp.bfloat16)
    blank = jnp.zeros((5, width), jnp.bfloat16)
    coords = jnp.concatenate(
        [(node_coords // 4).astype(jnp.bfloat16), blank, (node_coords % 4).astype(jnp.bfloat16), blank], axis=0
    )
    pack = jnp.concatenate([low, coords], axis=0)
    own = lax.all_to_all(jnp.broadcast_to(pack[None], (groups,) + pack.shape), "row", 0, 0)
    row_pack = lax.all_to_all(jnp.broadcast_to(coords[None], (stripes,) + coords.shape), "y", 0, 0)
    sibling = lax.ppermute(own, "c", [(0, 1), (1, 0)])
    partial = covariance_part(inv_range, row_pack, own)
    partial = covariance_part(inv_range, row_pack, sibling, partial)
    pieces = lax.all_to_all(partial, "y", 0, 0)
    slots = stripes * cores
    levels = -(-3 * (modes // 8) // slots)
    image, grams = call(
        gram_kernel,
        (
            jax.ShapeDtypeStruct((modes, width), jnp.float32),
            jax.ShapeDtypeStruct((slots, 8 * levels, 128), jnp.float32),
        ),
        pieces,
        mode_block,
    )
    grams = lax.all_to_all(grams, ("y", "c"), 0, 0)
    grams = call(spread_kernel, jax.ShapeDtypeStruct((groups, 8 * levels, 128), jnp.float32), grams)
    grams = lax.all_to_all(grams, "row", 0, 0)
    grams = call(spread_kernel, jax.ShapeDtypeStruct((slots, 8 * levels, 128), jnp.float32), grams)
    grams = lax.all_to_all(grams, ("y", "c"), 0, 0)
    basis, ritz = call(
        functools.partial(final_kernel, node_total),
        (
            jax.ShapeDtypeStruct((modes, width), jnp.float32),
            jax.ShapeDtypeStruct((modes, modes), jnp.float32),
        ),
        grams,
        image,
    )
    return (basis, ritz)


def solution(mesh):
    groups, slots = mesh.devices.shape
    parts = Mesh(mesh.devices.reshape(groups, slots // 2, 2), ("row", "y", "c"))
    nodes = P(None, ("row", "y", "c"))
    return jax.shard_map(
        body, mesh=parts, in_specs=(nodes, P(), nodes), out_specs=(nodes, P()), check_vma=False
    )
```

time: 618 us -> 164 us (0.27)
  waiting for transfers between devices: 331 us -> 0.01 us
  other arithmetic: 77.7 us -> 1.51 us
  matrix products: 74 us -> 0 us
  Pallas kernels: 0 us -> 41.8 us
  between operations: 14.2 us -> 0.73 us
  local copies, waits for them, and re-layouts: 7.58 us -> 0.21 us
  starting transfers between devices: 0.08 us -> 6.96 us
    psum x1 -> x0, waiting for transfers between devices: 269 us -> none  [body(): image_gram, cross = lax.psum((local_image, local_cross), ('row', 'col'))]
    all_gather x3 -> x0, blocking collectives: 112 us -> none  [the longest x1 43.4 us: body(): piece_pts = lax.all_gather(node_coords, 'row', axis=1, tiled=True)]
    all_to_all x0 -> x6, blocking collectives: none -> 112 us  [the longest x1 35.5 us: body(): lax.all_to_all(jnp.broadcast_to(pack[None], (groups,) + pack.shape), 'row...]
    dot_general x11 -> x0, matrix products: 71 us -> none  [the longest x8 66.8 us: one_block(): lax.dot_general(block_low, kernel, (((1,), (1,)), ((), ())), preferred_el...]
    reduce_scatter x1 -> x0, waiting for transfers between devices: 61.7 us -> none  [body(): lax.psum_scatter(finished, 'col', scatter_dimension=1, tiled=True)]
    pallas_call x0 -> x6, Pallas kernels: none -> 41.8 us  [the longest x2 31.9 us: covariance_part(): pl.pallas_call(functools.partial(cov_kernel, start is None, modes), out_s...]
    sub x8 -> x0, other arithmetic: 39.5 us -> none  [covariance(): diff = row_parts - col_parts]
    another operation x10 -> x0, other arithmetic: 34.9 us -> none  [the longest x3 9.45 us: body(): lower_modes = jnp.linalg.cholesky(mode_gram)]
  transfers between devices with their start and end apart: 2 -> 1, of which waited for: 2 -> 0; matrix products, arithmetic and copies ran while one was open for 0% -> 0% of each run, Pallas kernels for 0% -> 10%
where the time goes in v1:
time: 164 us; the launch traced here: 163 us
  blocking collectives  112 us (68%)
  Pallas kernels  41.8 us (25%)
  starting transfers between devices  6.96 us (4%)
    all_to_all x1, blocking collectives, body(): lax.all_to_all(jnp.broadcast_to(pack[None], (groups,) + pack.shape), 'row...  35.5 us
    pallas_call x2, Pallas kernels, covariance_part(): pl.pallas_call(functools.partial(cov_kernel, start is None, modes), out_s...  31.9 us
    all_to_all x2, blocking collectives, body(): grams = lax.all_to_all(grams, ('y', 'c'), 0, 0)  30.1 us
    all_to_all x1, blocking collectives, body(): grams = lax.all_to_all(grams, 'row', 0, 0)  17.6 us
    all_to_all x1, blocking collectives, body(): pieces = lax.all_to_all(partial, 'y', 0, 0)  15.6 us
    all_to_all x1, blocking collectives, body(): lax.all_to_all(jnp.broadcast_to(coords[None], (stripes,) + coords.shape),...  13.5 us
    pallas_call x4, Pallas kernels, call(): pl.pallas_call(kernel, out_shape=out_shape, compiler_params=PARAMS)(*args)  9.89 us
    ppermute x1, starting transfers between devices, body(): sibling = lax.ppermute(own, 'c', [(0, 1), (1, 0)])  6.96 us
  transfers between devices with their start and end apart: 1, of which 0 were waited for; matrix products, arithmetic and copies ran while one was open for 0% of the time, Pallas kernels for 10%

profile of v1, /device:TPU:1, one launch (start us, length us, event | category | flops | bytes accessed | tf_op | source)
XLA Modules:
  0.0 163.5 jit_solution(16780576787774573912)
XLA Ops:
  0.6 0.7 fusion
  1.3 0.8 convert_element_type.11
  2.1 0.1 concatenate.8
  2.2 0.1 broadcast_in_dim.8
  2.3 35.5 %all_to_all.30.col_ref = bf16[32,112,128]{2,1,0:T(8,128)(2,1)S(1)} all-to-all(bf16[32,112,128]{2,1,0:T(8,128)(2,1)S(1)} %broadcast_in_dim.8), channel_id=1, replica_groups=mesh['row'=32,'y'=8,'c'=2] {'row'}, dimensions={0} | all-to-all | bytes 1835008 | tf_op jit(solution)/shard_map/all_to_all | solution.py:185
  37.8 7.0 %collective-permute-start = (bf16[32,112,128]{2,1,0:T(8,128)(2,1)S(1)}, bf16[32,112,128]{2,1,0:T(8,128)(2,1)S(1)}, u32[]{:S(2)}, u32[]{:S(2)}) collective-permute-start(bf16[32,112,128]{2,1,0:T(8,128)(2,1)S(1)} %all_to_all.30.col_ref), channel_id=1, source_target_pairs={{0,1},{1,0},{2,3},{3,2},{4,5},{5,4},{6,7},{7,6},{8,9},{9,8},{10,11... | collective-permute-start | bytes 2752520 | tf_op jit(solution)/shard_map/ppermute | solution.py:187
  44.8 0.0 copy-start.1
  44.8 13.5 %all_to_all.31.row_ref = bf16[8,16,128]{2,1,0:T(8,128)(2,1)S(1)} all-to-all(bf16[8,16,128]{2,1,0:T(8,128)(2,1)S(1)} %broadcast_in_dim.7), channel_id=1, replica_groups=mesh['row'=32,'y'=8,'c'=2] {'y'}, dimensions={0} | all-to-all | bytes 65536 | tf_op jit(solution)/shard_map/all_to_all | solution.py:186
  58.3 0.0 copy-done.1
  58.3 16.0 %shard_map.50.refs_0_ = f32[8,96,128]{2,1,0:T(8,128)S(1)} custom-call(f32[3]{0:T(128)S(1)} %copy-done.1, bf16[8,16,128]{2,1,0:T(8,128)(2,1)S(1)} %all_to_all.31.row_ref, bf16[32,112,128]{2,1,0:T(8,128)(2,1)S(1)} %all_to_all.30.col_ref), custom_call_target="tpu_custom_call" | custom-call | flops 855638016 | bytes 393216 | tf_op jit(solution)/shard_map/pallas_call | solution.py:74
  74.3 0.0 collective-permute-done.col_ref
  74.3 16.0 %shard_map.51 = f32[8,96,128]{2,1,0:T(8,128)S(1)} custom-call(f32[3]{0:T(128)S(1)} %copy-done.1, bf16[8,16,128]{2,1,0:T(8,128)(2,1)S(1)} %all_to_all.31.row_ref, bf16[32,112,128]{2,1,0:T(8,128)(2,1)S(1)} %collective-permute-done.col_ref, f32[8,96,128]{2,1,0:T(8,128)S(1)} %shard_map.50.refs_0_), custom_call_target="tpu_custom_call" | custom-call | flops 855638016 | bytes 393216 | tf_op jit(solution)/shard_map/pallas_call | solution.py:74
  90.2 0.0 copy-start
  90.3 15.6 %all_to_all.32.part_ref = f32[8,96,128]{2,1,0:T(8,128)S(1)} all-to-all(f32[8,96,128]{2,1,0:T(8,128)S(1)} %shard_map.51), channel_id=1, replica_groups=mesh['row'=32,'y'=8,'c'=2] {'y'}, dimensions={0} | all-to-all | bytes 786432 | tf_op jit(solution)/shard_map/all_to_all | solution.py:190
  105.9 0.0 copy-done
  105.9 0.4 shard_map.52
  106.3 15.3 %all_to_all.33.part_ref = f32[16,24,128]{2,1,0:T(8,128)S(1)} all-to-all(f32[16,24,128]{2,1,0:T(8,128)S(1)} %get-tuple-element.4), channel_id=1, replica_groups=mesh['row'=32,'y'=8,'c'=2] {'y','c'}, dimensions={0} | all-to-all | bytes 393216 | tf_op jit(solution)/shard_map/all_to_all | solution.py:202
  121.7 17.6 %all_to_all.34.part_ref = f32[32,24,128]{2,1,0:T(8,128)S(1)} all-to-all(f32[32,24,128]{2,1,0:T(8,128)S(1)} %shard_map.53), channel_id=1, replica_groups=mesh['row'=32,'y'=8,'c'=2] {'row'}, dimensions={0} | all-to-all | bytes 786432 | tf_op jit(solution)/shard_map/all_to_all | solution.py:204
  139.3 14.7 %all_to_all.35.gram_ref = f32[16,24,128]{2,1,0:T(8,128)S(1)} all-to-all(f32[16,24,128]{2,1,0:T(8,128)S(1)} %shard_map.54), channel_id=1, replica_groups=mesh['row'=32,'y'=8,'c'=2] {'y','c'}, dimensions={0} | all-to-all | bytes 393216 | tf_op jit(solution)/shard_map/all_to_all | solution.py:206
  154.1 9.4 %shard_map.55 = (f32[96,128]{1,0:T(8,128)}, f32[96,96]{1,0:T(8,128)}) custom-call(f32[16,24,128]{2,1,0:T(8,128)S(1)} %all_to_all.35.gram_ref, f32[96,128]{1,0:T(8,128)S(1)} %get-tuple-element.5.image_ref), custom_call_target="tpu_custom_call" | custom-call | tf_op jit(solution)/shard_map/pallas_call | solution.py:172
  (5 shorter events, 0.1 us)
Async XLA Ops:
  37.8 36.5 %collective-permute-start = (bf16[32,112,128]{2,1,0:T(8,128)(2,1)S(1)}, bf16[32,112,128]{2,1,0:T(8,128)(2,1)S(1)}, u32[]{:S(2)}, u32[]{:S(2)}) collective-permute-start(bf16[32,112,128]{2,1,0:T(8,128)(2,1)S(1)} %all_to_all.30.col_ref), channel_id=1, source_target_pairs={{0,1},{1,0},{2,3},{3,2},{4,5},{5,4},{6,7},{7,6},{8,9},{9,8},{10,11... | collective-permute-start | bytes 2752520 | tf_op jit(solution)/shard_map/ppermute | solution.py:187
  44.8 13.5 %copy-start.1 = (f32[3]{0:T(128)S(1)}, f32[3]{0:T(128)}, u32[]{:S(2)}) copy-start(f32[3]{0:T(128)} %range_ref.3) | copy-start | bytes 40
  90.2 15.6 %copy-start = (f32[96,128]{1,0:T(8,128)S(1)}, f32[96,128]{1,0:T(8,128)}, u32[]{:S(2)}) copy-start(f32[96,128]{1,0:T(8,128)} %mode_ref.1) | copy-start | bytes 147460

commit v2 on v1

v2 whole, which is shorter than its diff:
```python
import functools
import math

import jax
import jax.numpy as jnp
from jax import lax
from jax.experimental import pallas as pl
from jax.experimental.pallas import tpu as pltpu
from jax.sharding import Mesh, PartitionSpec as P

NUGGET = 0.25
LOG2E = math.log2(math.e)
CENTRE = 512.0
HIGHEST = lax.Precision.HIGHEST
PARAMS = pltpu.CompilerParams(vmem_limit_bytes=48 * 1024 * 1024)


def scaled_coords(pack, scale):
    parts = pack.astype(jnp.float32)
    return (parts[0:8] * 4.0 + (parts[8:16] - CENTRE)) * scale


def scale_rows(range_ref):
    index = lax.broadcasted_iota(jnp.int32, (8, 128), 0)
    picked = jnp.where(
        index == 0,
        range_ref[0],
        jnp.where(index == 1, range_ref[1], jnp.where(index == 2, range_ref[2], 0.0)),
    )
    return picked * LOG2E


def cov_kernel(halves, modes, core_ref, range_ref, row_ref, col_ref, *refs):
    count = len(halves)
    start_refs, refs = refs[: len(refs) - 2 - count], refs[len(refs) - 2 - count :]
    out_refs, (rows, cols) = refs[:count], refs[count:]
    pieces, _, width = col_ref.shape
    dests = row_ref.shape[0] // 2
    scale = scale_rows(range_ref)
    low = jnp.concatenate([col_ref[piece, 0:modes, :] for piece in range(pieces)], axis=1)
    for piece in range(pieces):
        coords = scaled_coords(col_ref[piece, modes : modes + 16, :], scale).T
        for d in range(3):
            cols[d, piece * width : (piece + 1) * width, :] = jnp.broadcast_to(coords[:, d : d + 1], (width, width))
    for which, half in enumerate(halves):
        core = core_ref[0] if half == 0 else 1 - core_ref[0]
        for y in range(dests):
            rows[which, :, y * width : (y + 1) * width] = scaled_coords(row_ref[2 * y + core], scale)
        for pair in range(dests // 2):
            parts = []
            for y in (2 * pair, 2 * pair + 1):
                total = LOG2E * LOG2E
                for d in range(3):
                    delta = cols[d] - rows[which, d : d + 1, y * width : (y + 1) * width]
                    total = total + delta * delta
                parts.append(jnp.exp2(LOG2E - total * lax.rsqrt(total)).astype(jnp.bfloat16))
            update = jnp.dot(low, jnp.concatenate(parts, axis=1), preferred_element_type=jnp.float32)
            for y in range(2):
                term = update[:, y * width : (y + 1) * width]
                if start_refs:
                    term = term + start_refs[which][2 * pair + y]
                out_refs[which][2 * pair + y] = term


def covariance_part(core, inv_range, row_pack, col_pack, halves, starts=()):
    dests, _, width = row_pack.shape
    dests = dests // 2
    modes = col_pack.shape[1] - 16
    pairs = col_pack.shape[0] * dests * width * width * len(halves)
    vmem = pl.BlockSpec(memory_space=pltpu.VMEM)
    smem = pl.BlockSpec(memory_space=pltpu.SMEM)
    args = (core, inv_range, row_pack, col_pack) + tuple(starts)
    return pl.pallas_call(
        functools.partial(cov_kernel, halves, modes),
        out_shape=[jax.ShapeDtypeStruct((dests, modes, width), jnp.float32)] * len(halves),
        in_specs=[smem, smem] + [vmem] * (len(args) - 2),
        out_specs=[vmem] * len(halves),
        scratch_shapes=[
            pltpu.VMEM((len(halves), 8, dests * width), jnp.float32),
            pltpu.VMEM((3, col_pack.shape[0] * width, width), jnp.float32),
        ],
        input_output_aliases={4 + k: k for k in range(len(starts))},
        compiler_params=PARAMS,
        cost_estimate=pl.CostEstimate(
            flops=pairs * 2 * modes * 4, bytes_accessed=4 * dests * modes * width, transcendentals=2 * pairs
        ),
    )(*args)


def nt_dot(left, right):
    return lax.dot_general(
        left, right, (((1,), (1,)), ((), ())), precision=HIGHEST, preferred_element_type=jnp.float32
    )


def prepare_kernel(coord_ref, mode_ref, block_ref, row_ref):
    coords = coord_ref[...].astype(jnp.float32)
    high = jnp.floor(coords * 0.25)
    blank = jnp.zeros((5, coords.shape[1]), jnp.float32)
    pack = jnp.concatenate([high, blank, coords - 4.0 * high, blank], axis=0).astype(jnp.bfloat16)
    for k in range(row_ref.shape[0]):
        row_ref[k] = pack
    pack = jnp.concatenate([mode_ref[...].astype(jnp.bfloat16), pack], axis=0)
    for k in range(block_ref.shape[0]):
        block_ref[k] = pack


def gram_kernel(part_ref, mode_ref, image_ref, gram_ref):
    image = part_ref[0]
    for y in range(1, part_ref.shape[0]):
        image = image + part_ref[y]
    mode = mode_ref[...]
    image = image + NUGGET * mode
    image_ref[...] = image
    modes, width = image.shape
    third = modes // 3
    blank = jnp.zeros((third, width), jnp.float32)
    one, two = mode[third : 2 * third], mode[2 * third :]
    left = jnp.concatenate(
        [image, jnp.concatenate([one, two, blank], axis=0), jnp.concatenate([blank, blank, two], axis=0)], axis=1
    )
    right = jnp.concatenate(
        [
            jnp.concatenate([image, jnp.zeros((modes, 2 * width), jnp.float32)], axis=1),
            jnp.concatenate([blank, one, two], axis=1),
        ],
        axis=0,
    )
    grams = (nt_dot(left, right), nt_dot(mode, jnp.concatenate([image, mode[:third]], axis=0)))
    tiles, slots = modes // 8, gram_ref.shape[0]
    for which, gram in enumerate(grams):
        for t in range(tiles):
            level, slot = divmod(which * tiles + t, slots)
            gram_ref[slot, level * 8 : level * 8 + 8, :] = gram[t * 8 : t * 8 + 8, :]


def spread_kernel(part_ref, out_ref):
    total = part_ref[0]
    for k in range(1, part_ref.shape[0]):
        total = total + part_ref[k]
    for k in range(out_ref.shape[0]):
        out_ref[k] = total


def final_kernel(node_total, gram_ref, image_ref, basis_ref, ritz_ref):
    modes, width = image_ref.shape
    tiles = modes // 8
    slots = gram_ref.shape[0]

    def tile(which, t):
        level, slot = divmod(which * tiles + t, slots)
        return gram_ref[slot, level * 8 : level * 8 + 8, :] * (1.0 / node_total)

    lane = lax.broadcasted_iota(jnp.int32, (8, width), 1)
    row = lax.broadcasted_iota(jnp.int32, (8, width), 0)
    third = modes // 3
    lower = []
    for t in range(tiles):
        block = 8 * t // third
        value = pltpu.roll(tile(1, t), third, 1)
        if block >= 1:
            moved = pltpu.roll(tile(0, t - third // 8), 2 * third, 1)
            value = jnp.where(lane < third, value, moved)
        if block == 2:
            moved = pltpu.roll(tile(0, t), 3 * third, 1)
            value = jnp.where(lane < 2 * third, value, moved)
        lower.append(jnp.where(lane < (block + 1) * third, value, 0.0))
    upper = jnp.concatenate(lower + [jnp.zeros((width - modes, width), jnp.float32)], axis=0).T
    left = [
        [tile(0, t) for t in range(tiles)],
        [
            jnp.where(lane < (8 * t // third + 1) * third, lower[t], upper[8 * t : 8 * t + 8, :])
            for t in range(tiles)
        ],
    ]
    right = [
        [image_ref[t * 8 : t * 8 + 8, :] for t in range(tiles)],
        [jnp.where(lane == row + 8 * t, 1.0, 0.0) for t in range(tiles)],
    ]
    for k in range(modes):
        home, sub = divmod(k, 8)
        for m in range(2):
            a, b = left[m], right[m]
            spread = {t: jnp.broadcast_to(a[t][:, k : k + 1], (8, width)) for t in range(home, tiles)}
            inverse = 1.0 / spread[home][sub : sub + 1, :]
            row_a = jnp.broadcast_to(a[home][sub : sub + 1, :] * inverse, (8, width))
            row_b = jnp.broadcast_to(b[home][sub : sub + 1, :] * inverse, (8, width))
            for t in range(home, tiles):
                factor = spread[t]
                if t == home:
                    if sub == 7:
                        continue
                    factor = jnp.where(row > sub, factor, 0.0)
                a[t] = a[t] - factor * row_a
                b[t] = b[t] - factor * row_b

    def finish(m):
        rows = []
        for t in range(tiles):
            pivot = jnp.sum(jnp.where(lane == row + 8 * t, left[m][t], 0.0), axis=1, keepdims=True)
            rows.append(right[m][t] * (1.0 / jnp.sqrt(pivot)))
        return jnp.concatenate(rows, axis=0)

    basis_ref[...] = finish(0)
    inverse = finish(1)[:, 0:modes]
    cross = jnp.concatenate([tile(1, t) for t in range(tiles)], axis=0)[:, 0:modes]
    half = jnp.dot(inverse, cross, precision=HIGHEST, preferred_element_type=jnp.float32)
    ritz_ref[...] = nt_dot(half, inverse)


def call(kernel, out_shape, *args):
    return pl.pallas_call(kernel, out_shape=out_shape, compiler_params=PARAMS)(*args)


def body(node_coords, inv_range, mode_block):
    modes, width = mode_block.shape
    across, depth, stripes, cores = (lax.axis_size(axis) for axis in ("x", "z", "y", "c"))
    node_total = across * depth * stripes * cores * width
    slots = stripes * cores
    block, row_pack = call(
        prepare_kernel,
        (
            jax.ShapeDtypeStruct((depth, modes + 16, width), jnp.bfloat16),
            jax.ShapeDtypeStruct((slots, 16, width), jnp.bfloat16),
        ),
        node_coords,
        mode_block,
    )
    block = lax.all_to_all(block, "z", 0, 0)
    beside = lax.ppermute(block, "x", [(i, i ^ 1) for i in range(across)])
    row_pack = lax.all_to_all(row_pack, ("y", "c"), 0, 0)
    pair = jnp.concatenate([block, beside], axis=0)
    other = lax.ppermute(pair, "x", [(i, across - 1 - i) for i in range(across)])
    core = lax.axis_index("c").astype(jnp.int32)[None]
    shared = functools.partial(covariance_part, core, inv_range, row_pack)
    far, near = shared(block, (1, 0))
    far, near = shared(beside, (1, 0), (far, near))
    (far,) = shared(other, (1,), (far,))
    far = lax.ppermute(far, "c", [(0, 1), (1, 0)])
    (near,) = shared(other, (0,), (near,))
    pieces = lax.all_to_all(near + far, "y", 0, 0)
    slots = across * cores
    levels = -(-2 * (modes // 8) // slots)
    image, grams = call(
        gram_kernel,
        (
            jax.ShapeDtypeStruct((modes, width), jnp.float32),
            jax.ShapeDtypeStruct((slots, 8 * levels, width), jnp.float32),
        ),
        pieces,
        mode_block,
    )
    for axes, copies in ((("x", "c"), stripes), ("y", depth), ("z", slots)):
        grams = lax.all_to_all(grams, axes, 0, 0)
        grams = call(spread_kernel, jax.ShapeDtypeStruct((copies, 8 * levels, width), jnp.float32), grams)
    grams = lax.all_to_all(grams, ("x", "c"), 0, 0)
    basis, ritz = call(
        functools.partial(final_kernel, node_total),
        (
            jax.ShapeDtypeStruct((modes, width), jnp.float32),
            jax.ShapeDtypeStruct((modes, modes), jnp.float32),
        ),
        grams,
        image,
    )
    return (basis, ritz)


def solution(mesh):
    parts = Mesh(mesh.devices.reshape(4, mesh.devices.shape[0] // 4, -1, 2), ("x", "z", "y", "c"))
    nodes = P(None, ("x", "z", "y", "c"))
    return jax.shard_map(
        body, mesh=parts, in_specs=(nodes, P(), nodes), out_specs=(nodes, P()), check_vma=False
    )
```

time: 164 us -> 142 us (0.87)
  blocking collectives: 112 us -> 76.3 us
  starting transfers between devices: 6.96 us -> 20.5 us
  waiting for transfers between devices: 0.01 us -> 11.4 us
  Pallas kernels: 41.8 us -> 31.2 us
    all_to_all x6, blocking collectives: 112 us -> 76.3 us  [the longest x3 27.7 us: body(): grams = lax.all_to_all(grams, axes, 0, 0)]
    pallas_call x2 -> x4, Pallas kernels: 31.9 us -> 20.5 us  [covariance_part(): pl.pallas_call(functools.partial(cov_kernel, halves, modes), out_shape=[j...]
    all_to_all x0 -> x1, starting transfers between devices: none -> 10.9 us  [body(): row_pack = lax.all_to_all(row_pack, ('y', 'c'), 0, 0)]
    all_to_all x0 -> x1, waiting for transfers between devices: none -> 7.8 us  [body(): row_pack = lax.all_to_all(row_pack, ('y', 'c'), 0, 0)]
    ppermute x1 -> x3, waiting for transfers between devices: 0.01 us -> 3.64 us  [the longest x1 3.64 us: body(): beside = lax.ppermute(block, 'x', [(i, i ^ 1) for i in range(across)])]
    ppermute x1 -> x3, starting transfers between devices: 6.96 us -> 9.56 us  [the longest x1 4.39 us: body(): lax.ppermute(pair, 'x', [(i, across - 1 - i) for i in range(across)])]
    pallas_call x4 -> x6, Pallas kernels: 9.89 us -> 10.7 us  [call(): pl.pallas_call(kernel, out_shape=out_shape, compiler_params=PARAMS)(*args)]
  transfers between devices with their start and end apart: 1 -> 4, of which waited for: 0 -> 2; matrix products, arithmetic and copies ran while one was open for 0% -> 0% of each run, Pallas kernels for 10% -> 11%
where the time goes in v2:
time: 142 us
  blocking collectives  76.3 us (54%)
  Pallas kernels  31.2 us (22%)
  starting transfers between devices  20.5 us (14%)
  waiting for transfers between devices  11.4 us (8%)
  local copies, waits for them, and re-layouts  1.48 us (1%)
    all_to_all x3, blocking collectives, body(): grams = lax.all_to_all(grams, axes, 0, 0)  27.7 us
    pallas_call x4, Pallas kernels, covariance_part(): pl.pallas_call(functools.partial(cov_kernel, halves, modes), out_shape=[j...  20.5 us
    all_to_all x1, blocking collectives, body(): block = lax.all_to_all(block, 'z', 0, 0)  20.4 us
    all_to_all x1, blocking collectives, body(): pieces = lax.all_to_all(near + far, 'y', 0, 0)  17.7 us
    all_to_all x1, starting transfers between devices, body(): row_pack = lax.all_to_all(row_pack, ('y', 'c'), 0, 0)  10.9 us
    pallas_call x6, Pallas kernels, call(): pl.pallas_call(kernel, out_shape=out_shape, compiler_params=PARAMS)(*args)  10.7 us
    all_to_all x1, blocking collectives, body(): grams = lax.all_to_all(grams, ('x', 'c'), 0, 0)  10.5 us
    all_to_all x1, waiting for transfers between devices, body(): row_pack = lax.all_to_all(row_pack, ('y', 'c'), 0, 0)  7.8 us
  transfers between devices with their start and end apart: 4, of which 2 were waited for; matrix products, arithmetic and copies ran while one was open for 0% of the time, Pallas kernels for 11%

profile of v2, /device:TPU:1, one launch (start us, length us, event | category | flops | bytes accessed | tf_op | source)
XLA Modules:
  0.0 141.8 jit_solution(5494198156558366819)
XLA Ops:
  0.6 0.0 copy-start
  0.6 0.8 copy-done
  1.4 0.0 copy-start.2
  1.4 0.7 copy-done.2
  2.1 0.7 shard_map.50
  2.8 20.4 %all_to_all.35.col_ref = bf16[8,112,128]{2,1,0:T(8,128)(2,1)S(1)} all-to-all(bf16[8,112,128]{2,1,0:T(8,128)(2,1)S(1)} %get-tuple-element.11), channel_id=1, replica_groups=mesh['x'=4,'z'=8,'y'=8,'c'=2] {'z'}, dimensions={0} | all-to-all | bytes 458752 | tf_op jit(solution)/shard_map/all_to_all | solution.py:229
  23.2 3.1 %collective-permute-start = (bf16[8,112,128]{2,1,0:T(8,128)(2,1)S(1)}, bf16[8,112,128]{2,1,0:T(8,128)(2,1)S(1)}, u32[]{:S(2)}, u32[]{:S(2)}) collective-permute-start(bf16[8,112,128]{2,1,0:T(8,128)(2,1)S(1)} %all_to_all.35.col_ref), channel_id=1, source_target_pairs={{0,128},{128,0},{256,384},{384,256},{1,129},{129,1},{257,385},{385... | collective-permute-start | bytes 688136 | tf_op jit(solution)/shard_map/ppermute | solution.py:230
  26.3 3.6 %collective-permute-done.col_ref = bf16[8,112,128]{2,1,0:T(8,128)(2,1)S(1)} collective-permute-done((bf16[8,112,128]{2,1,0:T(8,128)(2,1)S(1)}, bf16[8,112,128]{2,1,0:T(8,128)(2,1)S(1)}, u32[]{:S(2)}, u32[]{:S(2)}) %collective-permute-start) | collective-permute-done | bytes 229408 | tf_op jit(solution)/shard_map/ppermute | solution.py:230
  30.0 4.4 %collective-permute-start.1 = (bf16[16,112,128]{2,1,0:T(8,128)(2,1)S(1)}, bf16[16,112,128]{2,1,0:T(8,128)(2,1)S(1)}, u32[]{:S(2)}, u32[]{:S(2)}) collective-permute-start(bf16[16,112,128]{2,1,0:T(8,128)(2,1)S(1)} %pad_maximum_fusion), channel_id=1, source_target_pairs={{0,384},{128,256},{256,128},{384,0},{1,385},{129,257},{257,129},{3... | collective-permute-start | bytes 1376264 | tf_op jit(solution)/shard_map/ppermute | solution.py:233
  34.4 10.9 %all-to-all-start = ((bf16[16,16,128]{2,1,0:T(8,128)(2,1)}), bf16[16,16,128]{2,1,0:T(8,128)(2,1)S(1)}, u32[]{:S(2)}, u32[]{:S(2)}) async-start(bf16[16,16,128]{2,1,0:T(8,128)(2,1)} %get-tuple-element.10), calls=%async_computation | async-start | bytes 131072 | tf_op jit(solution)/shard_map/all_to_all | solution.py:231
  45.3 0.0 copy-start.3
  45.3 7.8 %all-to-all-done.row_ref = bf16[16,16,128]{2,1,0:T(8,128)(2,1)S(1)} async-done(((bf16[16,16,128]{2,1,0:T(8,128)(2,1)}), bf16[16,16,128]{2,1,0:T(8,128)(2,1)S(1)}, u32[]{:S(2)}, u32[]{:S(2)}) %all-to-all-start) | async-done | bytes 65568 | tf_op jit(solution)/shard_map/all_to_all | solution.py:231
  53.1 0.0 copy-done.3
  53.1 5.0 %shard_map.51 = (f32[8,96,128]{2,1,0:T(8,128)S(1)}, f32[8,96,128]{2,1,0:T(8,128)S(1)}) custom-call(s32[1]{0:T(128)} %bitcast.core_ref, f32[3]{0:T(128)S(1)} %copy-done.3, bf16[16,16,128]{2,1,0:T(8,128)(2,1)S(1)} %all-to-all-done.row_ref, bf16[8,112,128]{2,1,0:T(8,128)(2,1)S(1)} %all_to_all.35.col_ref), custom_call_target="tpu_custom_call" | custom-call | flops 1610612736 | bytes 393216 | tf_op jit(solution)/shard_map/pallas_call | solution.py:73
  58.1 5.1 %shard_map.52 = (f32[8,96,128]{2,1,0:T(8,128)S(1)}, f32[8,96,128]{2,1,0:T(8,128)S(1)}) custom-call(s32[1]{0:T(128)} %bitcast.core_ref, f32[3]{0:T(128)S(1)} %copy-done.3, bf16[16,16,128]{2,1,0:T(8,128)(2,1)S(1)} %all-to-all-done.row_ref, bf16[8,112,128]{2,1,0:T(8,128)(2,1)S(1)} %collective-permute-done.col_ref, ...), custom_call_target="tpu_custom_call", output_to_operand_aliasing={{0}: (4, {}), {1}: (5, {})} | custom-call | flops 1610612736 | bytes 393216 | tf_op jit(solution)/shard_map/pallas_call | solution.py:73
  63.2 0.0 collective-permute-done.1.col_ref
  63.2 5.3 %shard_map.54 = f32[8,96,128]{2,1,0:T(8,128)S(1)} custom-call(s32[1]{0:T(128)} %bitcast.core_ref, f32[3]{0:T(128)S(1)} %copy-done.3, bf16[16,16,128]{2,1,0:T(8,128)(2,1)S(1)} %all-to-all-done.row_ref, bf16[16,112,128]{2,1,0:T(8,128)(2,1)S(1)} %collective-permute-done.1.col_ref, ...), custom_call_target="tpu_custom_call", output_to_operand_aliasing={{}: (4, {})} | custom-call | flops 1610612736 | bytes 393216 | tf_op jit(solution)/shard_map/pallas_call | solution.py:73
  68.5 2.1 %collective-permute-start.2 = (f32[8,96,128]{2,1,0:T(8,128)S(1)}, f32[8,96,128]{2,1,0:T(8,128)S(1)}, u32[]{:S(2)}, u32[]{:S(2)}) collective-permute-start(f32[8,96,128]{2,1,0:T(8,128)S(1)} %shard_map.54), channel_id=1, source_target_pairs={{0,1},{1,0},{2,3},{3,2},{4,5},{5,4},{6,7},{7,6},{8,9},{9,8},{10,11... | collective-permute-start | bytes 1179656 | tf_op jit(solution)/shard_map/ppermute | solution.py:239
  70.6 5.1 %shard_map.53 = f32[8,96,128]{2,1,0:T(8,128)S(1)} custom-call(s32[1]{0:T(128)} %bitcast.core_ref, f32[3]{0:T(128)S(1)} %copy-done.3, bf16[16,16,128]{2,1,0:T(8,128)(2,1)S(1)} %all-to-all-done.row_ref, bf16[16,112,128]{2,1,0:T(8,128)(2,1)S(1)} %collective-permute-done.1.col_ref, ...), custom_call_target="tpu_custom_call", output_to_operand_aliasing={{}: (4, {})} | custom-call | flops 1610612736 | bytes 393216 | tf_op jit(solution)/shard_map/pallas_call | solution.py:73
  75.7 0.0 collective-permute-done.2
  75.7 0.1 add.3
  75.8 0.0 copy-start.1
  75.8 17.7 %all_to_all.36.part_ref = f32[8,96,128]{2,1,0:T(8,128)S(1)} all-to-all(f32[8,96,128]{2,1,0:T(8,128)S(1)} %add.3), channel_id=1, replica_groups=mesh['x'=4,'z'=8,'y'=8,'c'=2] {'y'}, dimensions={0} | all-to-all | bytes 786432 | tf_op jit(solution)/shard_map/all_to_all | solution.py:241
  93.5 0.0 copy-done.1
  93.5 0.5 shard_map.55
  94.0 7.8 %all_to_all.37.part_ref = f32[8,24,128]{2,1,0:T(8,128)S(1)} all-to-all(f32[8,24,128]{2,1,0:T(8,128)S(1)} %get-tuple-element.16), channel_id=1, replica_groups=mesh['x'=4,'z'=8,'y'=8,'c'=2] {'x','c'}, dimensions={0} | all-to-all | bytes 196608 | tf_op jit(solution)/shard_map/all_to_all | solution.py:254
  101.8 9.8 %all_to_all.38.part_ref = f32[8,24,128]{2,1,0:T(8,128)S(1)} all-to-all(f32[8,24,128]{2,1,0:T(8,128)S(1)} %shard_map.56), channel_id=1, replica_groups=mesh['x'=4,'z'=8,'y'=8,'c'=2] {'y'}, dimensions={0} | all-to-all | bytes 196608 | tf_op jit(solution)/shard_map/all_to_all | solution.py:254
  111.7 10.1 %all_to_all.39.part_ref = f32[8,24,128]{2,1,0:T(8,128)S(1)} all-to-all(f32[8,24,128]{2,1,0:T(8,128)S(1)} %shard_map.57), channel_id=1, replica_groups=mesh['x'=4,'z'=8,'y'=8,'c'=2] {'z'}, dimensions={0} | all-to-all | bytes 196608 | tf_op jit(solution)/shard_map/all_to_all | solution.py:254
  121.7 10.5 %all_to_all.40.gram_ref = f32[8,24,128]{2,1,0:T(8,128)S(1)} all-to-all(f32[8,24,128]{2,1,0:T(8,128)S(1)} %shard_map.58), channel_id=1, replica_groups=mesh['x'=4,'z'=8,'y'=8,'c'=2] {'x','c'}, dimensions={0} | all-to-all | bytes 196608 | tf_op jit(solution)/shard_map/all_to_all | solution.py:256
  132.3 9.5 %shard_map.59 = (f32[96,128]{1,0:T(8,128)}, f32[96,96]{1,0:T(8,128)}) custom-call(f32[8,24,128]{2,1,0:T(8,128)S(1)} %all_to_all.40.gram_ref, f32[96,128]{1,0:T(8,128)S(1)} %get-tuple-element.17.image_ref), custom_call_target="tpu_custom_call" | custom-call | tf_op jit(solution)/shard_map/pallas_call | solution.py:212
  (4 shorter events, 0.1 us)
Async XLA Ops:
  0.6 0.8 copy-start
  1.4 0.7 copy-start.2
  23.2 6.8 %collective-permute-start = (bf16[8,112,128]{2,1,0:T(8,128)(2,1)S(1)}, bf16[8,112,128]{2,1,0:T(8,128)(2,1)S(1)}, u32[]{:S(2)}, u32[]{:S(2)}) collective-permute-start(bf16[8,112,128]{2,1,0:T(8,128)(2,1)S(1)} %all_to_all.35.col_ref), channel_id=1, source_target_pairs={{0,128},{128,0},{256,384},{384,256},{1,129},{129,1},{257,385},{385... | collective-permute-start | bytes 688136 | tf_op jit(solution)/shard_map/ppermute | solution.py:230
  30.0 33.2 %collective-permute-start.1 = (bf16[16,112,128]{2,1,0:T(8,128)(2,1)S(1)}, bf16[16,112,128]{2,1,0:T(8,128)(2,1)S(1)}, u32[]{:S(2)}, u32[]{:S(2)}) collective-permute-start(bf16[16,112,128]{2,1,0:T(8,128)(2,1)S(1)} %pad_maximum_fusion), channel_id=1, source_target_pairs={{0,384},{128,256},{256,128},{384,0},{1,385},{129,257},{257,129},{3... | collective-permute-start | bytes 1376264 | tf_op jit(solution)/shard_map/ppermute | solution.py:233
  34.4 18.7 %all-to-all-start = ((bf16[16,16,128]{2,1,0:T(8,128)(2,1)}), bf16[16,16,128]{2,1,0:T(8,128)(2,1)S(1)}, u32[]{:S(2)}, u32[]{:S(2)}) async-start(bf16[16,16,128]{2,1,0:T(8,128)(2,1)} %get-tuple-element.10), calls=%async_computation | async-start | bytes 131072 | tf_op jit(solution)/shard_map/all_to_all | solution.py:231
  45.3 7.8 %copy-start.3 = (f32[3]{0:T(128)S(1)}, f32[3]{0:T(128)}, u32[]{:S(2)}) copy-start(f32[3]{0:T(128)} %range_ref.7) | copy-start | bytes 40
  68.5 7.2 %collective-permute-start.2 = (f32[8,96,128]{2,1,0:T(8,128)S(1)}, f32[8,96,128]{2,1,0:T(8,128)S(1)}, u32[]{:S(2)}, u32[]{:S(2)}) collective-permute-start(f32[8,96,128]{2,1,0:T(8,128)S(1)} %shard_map.54), channel_id=1, source_target_pairs={{0,1},{1,0},{2,3},{3,2},{4,5},{5,4},{6,7},{7,6},{8,9},{9,8},{10,11... | collective-permute-start | bytes 1179656 | tf_op jit(solution)/shard_map/ppermute | solution.py:239
  75.8 17.7 %copy-start.1 = (f32[96,128]{1,0:T(8,128)S(1)}, f32[96,128]{1,0:T(8,128)}, u32[]{:S(2)}) copy-start(f32[96,128]{1,0:T(8,128)} %mode_ref.3) | copy-start | bytes 147460

commit v3 on v2

--- a/solution.py
+++ b/solution.py
@@ -93,16 +93,23 @@
     )
 
 
-def prepare_kernel(coord_ref, mode_ref, block_ref, row_ref):
+def pack_coords(coord_ref):
     coords = coord_ref[...].astype(jnp.float32)
     high = jnp.floor(coords * 0.25)
     blank = jnp.zeros((5, coords.shape[1]), jnp.float32)
-    pack = jnp.concatenate([high, blank, coords - 4.0 * high, blank], axis=0).astype(jnp.bfloat16)
-    for k in range(row_ref.shape[0]):
-        row_ref[k] = pack
-    pack = jnp.concatenate([mode_ref[...].astype(jnp.bfloat16), pack], axis=0)
-    for k in range(block_ref.shape[0]):
-        block_ref[k] = pack
+    return jnp.concatenate([high, blank, coords - 4.0 * high, blank], axis=0).astype(jnp.bfloat16)
+
+
+def row_kernel(coord_ref, out_ref):
+    pack = pack_coords(coord_ref)
+    for k in range(out_ref.shape[0]):
+        out_ref[k] = pack
+
+
+def block_kernel(coord_ref, mode_ref, out_ref):
+    pack = jnp.concatenate([mode_ref[...].astype(jnp.bfloat16), pack_coords(coord_ref)], axis=0)
+    for k in range(out_ref.shape[0]):
+        out_ref[k] = pack
 
 
 def gram_kernel(part_ref, mode_ref, image_ref, gram_ref):
@@ -128,6 +135,8 @@
     )
     grams = (nt_dot(left, right), nt_dot(mode, jnp.concatenate([image, mode[:third]], axis=0)))
     tiles, slots = modes // 8, gram_ref.shape[0]
+    for slot in range(2 * tiles % slots, slots):
+        gram_ref[slot, gram_ref.shape[1] - 8 :, :] = jnp.zeros((8, width), jnp.float32)
     for which, gram in enumerate(grams):
         for t in range(tiles):
             level, slot = divmod(which * tiles + t, slots)
@@ -177,32 +186,54 @@
         [image_ref[t * 8 : t * 8 + 8, :] for t in range(tiles)],
         [jnp.where(lane == row + 8 * t, 1.0, 0.0) for t in range(tiles)],
     ]
-    for k in range(modes):
+    for m in range(2):
+        picked = [jnp.where(lane == row + 8 * t, left[m][t], 0.0) for t in range(tiles)]
+        across = jnp.sum(functools.reduce(jnp.add, picked), axis=0, keepdims=True)
+        across = 1.0 / jnp.sqrt(jnp.where(lane[0:1] < modes, across, 1.0))
+        for t in range(tiles):
+            down = 1.0 / jnp.sqrt(jnp.sum(picked[t], axis=1, keepdims=True))
+            left[m][t] = left[m][t] * down * across
+            right[m][t] = right[m][t] * down
+
+    def spread_row(value, i):
+        return jnp.broadcast_to(value[i : i + 1, :], (8, width))
+
+    def spread_lane(value, k):
+        return jnp.broadcast_to(value[:, k : k + 1], (8, width))
+
+    done = [[None] * tiles, [None] * tiles]
+    for k in range(0, modes, 2):
         home, sub = divmod(k, 8)
+        near = [(spread_lane(left[m][home], k), spread_lane(left[m][home], k + 1)) for m in range(2)]
+        steps = []
         for m in range(2):
-            a, b = left[m], right[m]
-            spread = {t: jnp.broadcast_to(a[t][:, k : k + 1], (8, width)) for t in range(home, tiles)}
-            inverse = 1.0 / spread[home][sub : sub + 1, :]
-            row_a = jnp.broadcast_to(a[home][sub : sub + 1, :] * inverse, (8, width))
-            row_b = jnp.broadcast_to(b[home][sub : sub + 1, :] * inverse, (8, width))
-            for t in range(home, tiles):
-                factor = spread[t]
-                if t == home:
-                    if sub == 7:
-                        continue
-                    factor = jnp.where(row > sub, factor, 0.0)
-                a[t] = a[t] - factor * row_a
-                b[t] = b[t] - factor * row_b
-
-    def finish(m):
-        rows = []
-        for t in range(tiles):
-            pivot = jnp.sum(jnp.where(lane == row + 8 * t, left[m][t], 0.0), axis=1, keepdims=True)
-            rows.append(right[m][t] * (1.0 / jnp.sqrt(pivot)))
-        return jnp.concatenate(rows, axis=0)
-
-    basis_ref[...] = finish(0)
-    inverse = finish(1)[:, 0:modes]
+            first, second = near[m]
+            p, q, r = spread_row(first, sub), spread_row(first, sub + 1), spread_row(second, sub + 1)
+            a0, a1 = spread_row(left[m][home], sub), spread_row(left[m][home], sub + 1)
+            b0, b1 = spread_row(right[m][home], sub), spread_row(right[m][home], sub + 1)
+            scale = 1.0 / (p * r - q * q)
+            steps.append(
+                ((r * a0 - q * a1) * scale, (p * a1 - q * a0) * scale, (r * b0 - q * b1) * scale, (p * b1 - q * b0) * scale)
+            )
+            flat = 1.0 / p
+            ratio = q * flat
+            rows = jnp.where(row == sub, b0 * jnp.sqrt(flat), (b1 - ratio * b0) / jnp.sqrt(r - ratio * q))
+            done[m][home] = rows if sub == 0 else jnp.where(row >= sub, rows, done[m][home])
+        for t in range(home, tiles):
+            for m in range(2):
+                a, b = left[m], right[m]
+                if t > home:
+                    f0, f1 = spread_lane(a[t], k), spread_lane(a[t], k + 1)
+                elif sub < 6:
+                    f0, f1 = (jnp.where(row > sub + 1, part, 0.0) for part in near[m])
+                else:
+                    continue
+                a0, a1, b0, b1 = steps[m]
+                a[t] = a[t] - (f0 * a0 + f1 * a1)
+                b[t] = b[t] - (f0 * b0 + f1 * b1)
+
+    basis_ref[...] = jnp.concatenate(done[0], axis=0)
+    inverse = jnp.concatenate(done[1], axis=0)[:, 0:modes]
     cross = jnp.concatenate([tile(1, t) for t in range(tiles)], axis=0)[:, 0:modes]
     half = jnp.dot(inverse, cross, precision=HIGHEST, preferred_element_type=jnp.float32)
     ritz_ref[...] = nt_dot(half, inverse)
@@ -214,32 +245,27 @@
 
 def body(node_coords, inv_range, mode_block):
     modes, width = mode_block.shape
-    across, depth, stripes, cores = (lax.axis_size(axis) for axis in ("x", "z", "y", "c"))
-    node_total = across * depth * stripes * cores * width
-    slots = stripes * cores
-    block, row_pack = call(
-        prepare_kernel,
-        (
-            jax.ShapeDtypeStruct((depth, modes + 16, width), jnp.bfloat16),
-            jax.ShapeDtypeStruct((slots, 16, width), jnp.bfloat16),
-        ),
-        node_coords,
-        mode_block,
-    )
-    block = lax.all_to_all(block, "z", 0, 0)
-    beside = lax.ppermute(block, "x", [(i, i ^ 1) for i in range(across)])
-    row_pack = lax.all_to_all(row_pack, ("y", "c"), 0, 0)
-    pair = jnp.concatenate([block, beside], axis=0)
-    other = lax.ppermute(pair, "x", [(i, across - 1 - i) for i in range(across)])
+    near_axes, far_axes, last = ("xl", "zl", "yl"), ("zh", "yh"), "xh"
+    count = {axis: lax.axis_size(axis) for axis in near_axes + far_axes + (last, "c")}
+    dests, sources = (math.prod(count[axis] for axis in axes) for axes in (near_axes, far_axes))
+    node_total = math.prod(count.values()) * width
+    row_pack = call(row_kernel, jax.ShapeDtypeStruct((2 * dests, 16, width), jnp.bfloat16), node_coords)
+    row_pack = lax.all_to_all(row_pack, near_axes + ("c",), 0, 0)
+    block = call(
+        block_kernel, jax.ShapeDtypeStruct((sources, modes + 16, width), jnp.bfloat16), node_coords, mode_block
+    )
+    block, row_pack = lax.optimization_barrier((block, row_pack))
+    block = lax.all_to_all(block, far_axes, 0, 0)
+    other = lax.ppermute(block, last, [(0, 1), (1, 0)])
     core = lax.axis_index("c").astype(jnp.int32)[None]
     shared = functools.partial(covariance_part, core, inv_range, row_pack)
     far, near = shared(block, (1, 0))
-    far, near = shared(beside, (1, 0), (far, near))
     (far,) = shared(other, (1,), (far,))
     far = lax.ppermute(far, "c", [(0, 1), (1, 0)])
     (near,) = shared(other, (0,), (near,))
-    pieces = lax.all_to_all(near + far, "y", 0, 0)
-    slots = across * cores
+    pieces = lax.all_to_all(near + far, near_axes, 0, 0)
+    split_axes = (last,) + near_axes + ("c",)
+    slots = math.prod(count[axis] for axis in split_axes)
     levels = -(-2 * (modes // 8) // slots)
     image, grams = call(
         gram_kernel,
@@ -250,10 +276,10 @@
         pieces,
         mode_block,
     )
-    for axes, copies in ((("x", "c"), stripes), ("y", depth), ("z", slots)):
+    for axes, copies in ((split_axes, sources), (far_axes, slots)):
         grams = lax.all_to_all(grams, axes, 0, 0)
         grams = call(spread_kernel, jax.ShapeDtypeStruct((copies, 8 * levels, width), jnp.float32), grams)
-    grams = lax.all_to_all(grams, ("x", "c"), 0, 0)
+    grams = lax.all_to_all(grams, split_axes, 0, 0)
     basis, ritz = call(
         functools.partial(final_kernel, node_total),
         (
@@ -267,8 +293,9 @@
 
 
 def solution(mesh):
-    parts = Mesh(mesh.devices.reshape(4, mesh.devices.shape[0] // 4, -1, 2), ("x", "z", "y", "c"))
-    nodes = P(None, ("x", "z", "y", "c"))
+    axes = ("xh", "xl", "zh", "zl", "yh", "yl", "c")
+    parts = Mesh(mesh.devices.reshape(2, 2, 4, 2, 4, 2, 2), axes)
+    nodes = P(None, axes)
     return jax.shard_map(
         body, mesh=parts, in_specs=(nodes, P(), nodes), out_specs=(nodes, P()), check_vma=False
     )

time: 142 us -> 135 us (0.951)
  waiting for transfers between devices: 11.4 us -> 5.09 us
  blocking collectives: 76.3 us -> 79.3 us
  Pallas kernels: 31.2 us -> 29.3 us
    ppermute x2 -> x1, waiting for transfers between devices: 3.64 us -> 0.01 us  [body(): other = lax.ppermute(block, last, [(0, 1), (1, 0)])]
    ppermute x2 -> x1, starting transfers between devices: 7.49 us -> 4.35 us  [body(): other = lax.ppermute(block, last, [(0, 1), (1, 0)])]
    all_to_all x1, waiting for transfers between devices: 7.8 us -> 5.08 us  [body(): row_pack = lax.all_to_all(row_pack, near_axes + ('c',), 0, 0)]
    ppermute x1, starting transfers between devices: 2.07 us -> 4.61 us  [body(): far = lax.ppermute(far, 'c', [(0, 1), (1, 0)])]
    all_to_all x3 -> x2, blocking collectives: 27.7 us -> 29.9 us  [body(): grams = lax.all_to_all(grams, axes, 0, 0)]
    pallas_call x4 -> x3, Pallas kernels: 20.5 us -> 19.7 us  [covariance_part(): pl.pallas_call(functools.partial(cov_kernel, halves, modes), out_shape=[j...]
  transfers between devices with their start and end apart: 4 -> 3, of which waited for: 2 -> 1; matrix products, arithmetic and copies ran while one was open for 0% -> 0% of each run, Pallas kernels for 11% -> 11%
where the time goes in v3:
time: 135 us
  blocking collectives  79.3 us (59%)
  Pallas kernels  29.3 us (22%)
  starting transfers between devices  19.2 us (14%)
  waiting for transfers between devices  5.09 us (4%)
    all_to_all x2, blocking collectives, body(): grams = lax.all_to_all(grams, axes, 0, 0)  29.9 us
    all_to_all x1, blocking collectives, body(): block = lax.all_to_all(block, far_axes, 0, 0)  27.1 us
    pallas_call x3, Pallas kernels, covariance_part(): pl.pallas_call(functools.partial(cov_kernel, halves, modes), out_shape=[j...  19.7 us
    all_to_all x1, blocking collectives, body(): grams = lax.all_to_all(grams, split_axes, 0, 0)  11.7 us
    all_to_all x1, blocking collectives, body(): pieces = lax.all_to_all(near + far, near_axes, 0, 0)  10.5 us
    all_to_all x1, starting transfers between devices, body(): row_pack = lax.all_to_all(row_pack, near_axes + ('c',), 0, 0)  10.3 us
    pallas_call x6, Pallas kernels, call(): pl.pallas_call(kernel, out_shape=out_shape, compiler_params=PARAMS)(*args)  9.58 us
    all_to_all x1, waiting for transfers between devices, body(): row_pack = lax.all_to_all(row_pack, near_axes + ('c',), 0, 0)  5.08 us
  transfers between devices with their start and end apart: 3, of which 1 were waited for; matrix products, arithmetic and copies ran while one was open for 0% of the time, Pallas kernels for 11%

profile of v3, /device:TPU:1, one launch (start us, length us, event | category | flops | bytes accessed | tf_op | source)
XLA Modules:
  0.0 135.0 jit_solution(15838560515846574895)
XLA Ops:
  0.6 0.0 copy-start.1
  0.6 0.7 copy-done.1
  1.3 0.6 shard_map.51
  1.9 0.0 copy-start
  1.9 0.0 copy-start.2
  1.9 10.3 %all-to-all-start = ((bf16[16,16,128]{2,1,0:T(8,128)(2,1)}), bf16[16,16,128]{2,1,0:T(8,128)(2,1)S(1)}, u32[]{:S(2)}, u32[]{:S(2)}) async-start(bf16[16,16,128]{2,1,0:T(8,128)(2,1)} %shard_map.51), calls=%async_computation | async-start | bytes 131072 | tf_op jit(solution)/shard_map/all_to_all | solution.py:253
  12.2 0.0 copy-done
  12.2 0.0 copy-done.2
  12.3 5.1 %all-to-all-done.row_ref = bf16[16,16,128]{2,1,0:T(8,128)(2,1)S(1)} async-done(((bf16[16,16,128]{2,1,0:T(8,128)(2,1)}), bf16[16,16,128]{2,1,0:T(8,128)(2,1)S(1)}, u32[]{:S(2)}, u32[]{:S(2)}) %all-to-all-start) | async-done | bytes 65568 | tf_op jit(solution)/shard_map/all_to_all | solution.py:253
  17.4 27.1 %all_to_all.30.col_ref = bf16[16,112,128]{2,1,0:T(8,128)(2,1)S(1)} all-to-all(bf16[16,112,128]{2,1,0:T(8,128)(2,1)S(1)} %shard_map.50), channel_id=1, replica_groups=mesh['xh'=2,'xl'=2,'zh'=4,'zl'=2,'yh'=4,'yl'=2,'c'=2] {'zh','yh'}, dimensions={0} | all-to-all | bytes 917504 | tf_op jit(solution)/shard_map/all_to_all | solution.py:258
  44.5 4.3 %collective-permute-start = (bf16[16,112,128]{2,1,0:T(8,128)(2,1)S(1)}, bf16[16,112,128]{2,1,0:T(8,128)(2,1)S(1)}, u32[]{:S(2)}, u32[]{:S(2)}) collective-permute-start(bf16[16,112,128]{2,1,0:T(8,128)(2,1)S(1)} %all_to_all.30.col_ref), channel_id=1, source_target_pairs={{0,256},{256,0},{1,257},{257,1},{2,258},{258,2},{3,259},{259,3},{4... | collective-permute-start | bytes 1376264 | tf_op jit(solution)/shard_map/ppermute | solution.py:259
  48.9 0.0 copy-start.3
  48.9 0.6 copy-done.3
  49.5 9.3 %shard_map.52 = (f32[8,96,128]{2,1,0:T(8,128)S(1)}, f32[8,96,128]{2,1,0:T(8,128)S(1)}) custom-call(s32[1]{0:T(128)} %bitcast.core_ref, f32[3]{0:T(128)S(1)} %copy-done.3, bf16[16,16,128]{2,1,0:T(8,128)(2,1)S(1)} %all-to-all-done.row_ref, bf16[16,112,128]{2,1,0:T(8,128)(2,1)S(1)} %all_to_all.30.col_ref), custom_call_target="tpu_custom_call" | custom-call | flops 3221225472 | bytes 393216 | tf_op jit(solution)/shard_map/pallas_call | solution.py:73
  58.9 0.0 collective-permute-done.col_ref
  58.9 5.3 %shard_map.54 = f32[8,96,128]{2,1,0:T(8,128)S(1)} custom-call(s32[1]{0:T(128)} %bitcast.core_ref, f32[3]{0:T(128)S(1)} %copy-done.3, bf16[16,16,128]{2,1,0:T(8,128)(2,1)S(1)} %all-to-all-done.row_ref, bf16[16,112,128]{2,1,0:T(8,128)(2,1)S(1)} %collective-permute-done.col_ref, f32[8,96,128]{2,1,0:T(8,128)S(1)} %get-tuple-element.11.refs_0_), custom_call_target="tpu_custom_call", output_to_operand_aliasing={{}: (4, {})} | custom-call | flops 1610612736 | bytes 393216 | tf_op jit(solution)/shard_map/pallas_call | solution.py:73
  64.2 4.6 %collective-permute-start.1 = (f32[8,96,128]{2,1,0:T(8,128)S(1)}, f32[8,96,128]{2,1,0:T(8,128)S(1)}, u32[]{:S(2)}, u32[]{:S(2)}) collective-permute-start(f32[8,96,128]{2,1,0:T(8,128)S(1)} %shard_map.54), channel_id=1, source_target_pairs={{0,1},{1,0},{2,3},{3,2},{4,5},{5,4},{6,7},{7,6},{8,9},{9,8},{10,11... | collective-permute-start | bytes 1179656 | tf_op jit(solution)/shard_map/ppermute | solution.py:264
  68.8 5.1 %shard_map.53 = f32[8,96,128]{2,1,0:T(8,128)S(1)} custom-call(s32[1]{0:T(128)} %bitcast.core_ref, f32[3]{0:T(128)S(1)} %copy-done.3, bf16[16,16,128]{2,1,0:T(8,128)(2,1)S(1)} %all-to-all-done.row_ref, bf16[16,112,128]{2,1,0:T(8,128)(2,1)S(1)} %collective-permute-done.col_ref, f32[8,96,128]{2,1,0:T(8,128)S(1)} %get-tuple-element.10.refs_0_), custom_call_target="tpu_custom_call", output_to_operand_aliasing={{}: (4, {})} | custom-call | flops 1610612736 | bytes 393216 | tf_op jit(solution)/shard_map/pallas_call | solution.py:73
  73.9 0.0 collective-permute-done.1
  73.9 0.1 add.3
  74.0 10.5 %all_to_all.31.part_ref = f32[8,96,128]{2,1,0:T(8,128)S(1)} all-to-all(f32[8,96,128]{2,1,0:T(8,128)S(1)} %add.3), channel_id=1, replica_groups=mesh['xh'=2,'xl'=2,'zh'=4,'zl'=2,'yh'=4,'yl'=2,'c'=2] {'xl','zl','yl'}, dimensions={0} | all-to-all | bytes 786432 | tf_op jit(solution)/shard_map/all_to_all | solution.py:266
  84.5 0.5 shard_map.55
  85.0 12.0 %all_to_all.32.part_ref = f32[32,8,128]{2,1,0:T(8,128)S(1)} all-to-all(f32[32,8,128]{2,1,0:T(8,128)S(1)} %get-tuple-element.12), channel_id=1, replica_groups=mesh['xh'=2,'xl'=2,'zh'=4,'zl'=2,'yh'=4,'yl'=2,'c'=2] {'xh','xl','zl','y..., dimensions={0} | all-to-all | bytes 262144 | tf_op jit(solution)/shard_map/all_to_all | solution.py:280
  97.0 17.9 %all_to_all.33.part_ref = f32[16,8,128]{2,1,0:T(8,128)S(1)} all-to-all(f32[16,8,128]{2,1,0:T(8,128)S(1)} %shard_map.56), channel_id=1, replica_groups=mesh['xh'=2,'xl'=2,'zh'=4,'zl'=2,'yh'=4,'yl'=2,'c'=2] {'zh','yh'}, dimensions={0} | all-to-all | bytes 131072 | tf_op jit(solution)/shard_map/all_to_all | solution.py:280
  114.9 11.7 %all_to_all.34.gram_ref = f32[32,8,128]{2,1,0:T(8,128)S(1)} all-to-all(f32[32,8,128]{2,1,0:T(8,128)S(1)} %shard_map.57), channel_id=1, replica_groups=mesh['xh'=2,'xl'=2,'zh'=4,'zl'=2,'yh'=4,'yl'=2,'c'=2] {'xh','xl','zl','y..., dimensions={0} | all-to-all | bytes 262144 | tf_op jit(solution)/shard_map/all_to_all | solution.py:282
  126.7 8.3 %shard_map.58 = (f32[96,128]{1,0:T(8,128)}, f32[96,96]{1,0:T(8,128)}) custom-call(f32[32,8,128]{2,1,0:T(8,128)S(1)} %all_to_all.34.gram_ref, f32[96,128]{1,0:T(8,128)S(1)} %get-tuple-element.13.image_ref), custom_call_target="tpu_custom_call" | custom-call | tf_op jit(solution)/shard_map/pallas_call | solution.py:243
  (3 shorter events, 0.1 us)
Async XLA Ops:
  0.6 0.7 copy-start.1
  1.9 10.3 %copy-start = (f32[96,128]{1,0:T(8,128)S(1)}, f32[96,128]{1,0:T(8,128)}, u32[]{:S(2)}) copy-start(f32[96,128]{1,0:T(8,128)} %mode_ref.3) | copy-start | bytes 147460
  1.9 10.3 %copy-start.2 = (s32[3,128]{1,0:T(4,128)S(1)}, s32[3,128]{1,0:T(4,128)}, u32[]{:S(2)}) copy-start(s32[3,128]{1,0:T(4,128)} %coord_ref.3) | copy-start | bytes 4612
  1.9 15.4 %all-to-all-start = ((bf16[16,16,128]{2,1,0:T(8,128)(2,1)}), bf16[16,16,128]{2,1,0:T(8,128)(2,1)S(1)}, u32[]{:S(2)}, u32[]{:S(2)}) async-start(bf16[16,16,128]{2,1,0:T(8,128)(2,1)} %shard_map.51), calls=%async_computation | async-start | bytes 131072 | tf_op jit(solution)/shard_map/all_to_all | solution.py:253
  44.5 14.3 %collective-permute-start = (bf16[16,112,128]{2,1,0:T(8,128)(2,1)S(1)}, bf16[16,112,128]{2,1,0:T(8,128)(2,1)S(1)}, u32[]{:S(2)}, u32[]{:S(2)}) collective-permute-start(bf16[16,112,128]{2,1,0:T(8,128)(2,1)S(1)} %all_to_all.30.col_ref), channel_id=1, source_target_pairs={{0,256},{256,0},{1,257},{257,1},{2,258},{258,2},{3,259},{259,3},{4... | collective-permute-start | bytes 1376264 | tf_op jit(solution)/shard_map/ppermute | solution.py:259
  48.9 0.7 copy-start.3
  64.2 9.7 %collective-permute-start.1 = (f32[8,96,128]{2,1,0:T(8,128)S(1)}, f32[8,96,128]{2,1,0:T(8,128)S(1)}, u32[]{:S(2)}, u32[]{:S(2)}) collective-permute-start(f32[8,96,128]{2,1,0:T(8,128)S(1)} %shard_map.54), channel_id=1, source_target_pairs={{0,1},{1,0},{2,3},{3,2},{4,5},{5,4},{6,7},{7,6},{8,9},{9,8},{10,11... | collective-permute-start | bytes 1179656 | tf_op jit(solution)/shard_map/ppermute | solution.py:264

commit v4 on v3

--- a/solution.py
+++ b/solution.py
@@ -245,8 +245,9 @@
 
 def body(node_coords, inv_range, mode_block):
     modes, width = mode_block.shape
-    near_axes, far_axes, last = ("xl", "zl", "yl"), ("zh", "yh"), "xh"
-    count = {axis: lax.axis_size(axis) for axis in near_axes + far_axes + (last, "c")}
+    near_axes, far_axes, ring = ("xh", "xl", "yl"), ("zh", "zl"), "yh"
+    split_axes, joint_axes = ("xh", "xl", "zl", "yl", "c"), ("zh", "yh")
+    count = {axis: lax.axis_size(axis) for axis in near_axes + far_axes + (ring, "c")}
     dests, sources = (math.prod(count[axis] for axis in axes) for axes in (near_axes, far_axes))
     node_total = math.prod(count.values()) * width
     row_pack = call(row_kernel, jax.ShapeDtypeStruct((2 * dests, 16, width), jnp.bfloat16), node_coords)
@@ -256,16 +257,19 @@
     )
     block, row_pack = lax.optimization_barrier((block, row_pack))
     block = lax.all_to_all(block, far_axes, 0, 0)
-    other = lax.ppermute(block, last, [(0, 1), (1, 0)])
+    around = count[ring]
+    order = [1, around - 1] + list(range(2, around - 1))
+    others = [lax.ppermute(block, ring, [(i, (i + shift) % around) for i in range(around)]) for shift in order]
     core = lax.axis_index("c").astype(jnp.int32)[None]
     shared = functools.partial(covariance_part, core, inv_range, row_pack)
     far, near = shared(block, (1, 0))
-    (far,) = shared(other, (1,), (far,))
+    for other in others[:-1]:
+        far, near = shared(other, (1, 0), (far, near))
+    (far,) = shared(others[-1], (1,), (far,))
     far = lax.ppermute(far, "c", [(0, 1), (1, 0)])
-    (near,) = shared(other, (0,), (near,))
+    (near,) = shared(others[-1], (0,), (near,))
     pieces = lax.all_to_all(near + far, near_axes, 0, 0)
-    split_axes = (last,) + near_axes + ("c",)
-    slots = math.prod(count[axis] for axis in split_axes)
+    slots, joined = (math.prod(count[axis] for axis in axes) for axes in (split_axes, joint_axes))
     levels = -(-2 * (modes // 8) // slots)
     image, grams = call(
         gram_kernel,
@@ -276,7 +280,7 @@
         pieces,
         mode_block,
     )
-    for axes, copies in ((split_axes, sources), (far_axes, slots)):
+    for axes, copies in ((split_axes, joined), (joint_axes, slots)):
         grams = lax.all_to_all(grams, axes, 0, 0)
         grams = call(spread_kernel, jax.ShapeDtypeStruct((copies, 8 * levels, width), jnp.float32), grams)
     grams = lax.all_to_all(grams, split_axes, 0, 0)

time: 135 us -> 141 us (1.044)
  starting transfers between devices: 19.2 us -> 27.3 us
  blocking collectives: 79.3 us -> 73 us
  waiting for transfers between devices: 5.09 us -> 7.64 us
  Pallas kernels: 29.3 us -> 30.9 us
    all_to_all x1, blocking collectives: 27.1 us -> 16.5 us  [body(): block = lax.all_to_all(block, far_axes, 0, 0)]
    ppermute x1 -> x3, starting transfers between devices: 4.35 us -> 13.9 us  [body(): lax.ppermute(block, ring, [(i, (i + shift) % around) for i in range(aroun...]
    all_to_all x2, blocking collectives: 29.9 us -> 33.2 us  [body(): grams = lax.all_to_all(grams, axes, 0, 0)]
    ppermute x1 -> x3, waiting for transfers between devices: 0.01 us -> 1.79 us  [body(): lax.ppermute(block, ring, [(i, (i + shift) % around) for i in range(aroun...]
    pallas_call x3 -> x5, Pallas kernels: 19.7 us -> 21.4 us  [covariance_part(): pl.pallas_call(functools.partial(cov_kernel, halves, modes), out_shape=[j...]
    ppermute x1, starting transfers between devices: 4.61 us -> 3.04 us  [body(): far = lax.ppermute(far, 'c', [(0, 1), (1, 0)])]
  transfers between devices with their start and end apart: 3 -> 5, of which waited for: 1 -> 2; matrix products, arithmetic and copies ran while one was open for 0% -> 0% of each run, Pallas kernels for 11% -> 13%
where the time goes in v4:
time: 141 us; the launch traced here: 140 us
  blocking collectives  73 us (52%)
  Pallas kernels  30.9 us (22%)
  starting transfers between devices  27.3 us (19%)
  waiting for transfers between devices  7.64 us (5%)
    all_to_all x2, blocking collectives, body(): grams = lax.all_to_all(grams, axes, 0, 0)  33.2 us
    pallas_call x5, Pallas kernels, covariance_part(): pl.pallas_call(functools.partial(cov_kernel, halves, modes), out_shape=[j...  21.4 us
    all_to_all x1, blocking collectives, body(): block = lax.all_to_all(block, far_axes, 0, 0)  16.5 us
    ppermute x3, starting transfers between devices, body(): lax.ppermute(block, ring, [(i, (i + shift) % around) for i in range(aroun...  13.9 us
    all_to_all x1, blocking collectives, body(): grams = lax.all_to_all(grams, split_axes, 0, 0)  11.7 us
    all_to_all x1, blocking collectives, body(): pieces = lax.all_to_all(near + far, near_axes, 0, 0)  11.6 us
    all_to_all x1, starting transfers between devices, body(): row_pack = lax.all_to_all(row_pack, near_axes + ('c',), 0, 0)  10.3 us
    pallas_call x6, Pallas kernels, call(): pl.pallas_call(kernel, out_shape=out_shape, compiler_params=PARAMS)(*args)  9.56 us
  transfers between devices with their start and end apart: 5, of which 2 were waited for; matrix products, arithmetic and copies ran while one was open for 0% of the time, Pallas kernels for 13%

profile of v4, /device:TPU:1, one launch (start us, length us, event | category | flops | bytes accessed | tf_op | source)
XLA Modules:
  0.0 140.4 jit_solution(2890116939452885136)
XLA Ops:
  0.6 0.0 copy-start.1
  0.6 0.7 copy-done.1
  1.3 0.6 shard_map.51
  1.9 0.0 copy-start
  1.9 0.0 copy-start.2
  2.0 10.3 %all-to-all-start = ((bf16[16,16,128]{2,1,0:T(8,128)(2,1)}), bf16[16,16,128]{2,1,0:T(8,128)(2,1)S(1)}, u32[]{:S(2)}, u32[]{:S(2)}) async-start(bf16[16,16,128]{2,1,0:T(8,128)(2,1)} %shard_map.51), calls=%async_computation | async-start | bytes 131072 | tf_op jit(solution)/shard_map/all_to_all | solution.py:254
  12.2 0.0 copy-done
  12.2 0.0 copy-done.2
  12.3 5.8 %all-to-all-done.row_ref = bf16[16,16,128]{2,1,0:T(8,128)(2,1)S(1)} async-done(((bf16[16,16,128]{2,1,0:T(8,128)(2,1)}), bf16[16,16,128]{2,1,0:T(8,128)(2,1)S(1)}, u32[]{:S(2)}, u32[]{:S(2)}) %all-to-all-start) | async-done | bytes 65568 | tf_op jit(solution)/shard_map/all_to_all | solution.py:254
  18.1 16.5 %all_to_all.30.col_ref = bf16[8,112,128]{2,1,0:T(8,128)(2,1)S(1)} all-to-all(bf16[8,112,128]{2,1,0:T(8,128)(2,1)S(1)} %shard_map.50), channel_id=1, replica_groups=mesh['xh'=2,'xl'=2,'zh'=4,'zl'=2,'yh'=4,'yl'=2,'c'=2] {'zh','zl'}, dimensions={0} | all-to-all | bytes 458752 | tf_op jit(solution)/shard_map/all_to_all | solution.py:259
  34.6 4.2 %collective-permute-start.2 = (bf16[8,112,128]{2,1,0:T(8,128)(2,1)S(1)}, bf16[8,112,128]{2,1,0:T(8,128)(2,1)S(1)}, u32[]{:S(2)}, u32[]{:S(2)}) collective-permute-start(bf16[8,112,128]{2,1,0:T(8,128)(2,1)S(1)} %all_to_all.30.col_ref), channel_id=1, source_target_pairs={{0,4},{4,8},{8,12},{12,0},{1,5},{5,9},{9,13},{13,1},{2,6},{6,10},{... | collective-permute-start | bytes 688136 | tf_op jit(solution)/shard_map/ppermute | solution.py:262
  38.8 0.0 copy-start.3
  38.9 3.2 %collective-permute-start.1 = (bf16[8,112,128]{2,1,0:T(8,128)(2,1)S(1)}, bf16[8,112,128]{2,1,0:T(8,128)(2,1)S(1)}, u32[]{:S(2)}, u32[]{:S(2)}) collective-permute-start(bf16[8,112,128]{2,1,0:T(8,128)(2,1)S(1)} %all_to_all.30.col_ref), channel_id=1, source_target_pairs={{0,12},{4,0},{8,4},{12,8},{1,13},{5,1},{9,5},{13,9},{2,14},{6,2},{... | collective-permute-start | bytes 688136 | tf_op jit(solution)/shard_map/ppermute | solution.py:262
  42.0 6.6 %collective-permute-start = (bf16[8,112,128]{2,1,0:T(8,128)(2,1)S(1)}, bf16[8,112,128]{2,1,0:T(8,128)(2,1)S(1)}, u32[]{:S(2)}, u32[]{:S(2)}) collective-permute-start(bf16[8,112,128]{2,1,0:T(8,128)(2,1)S(1)} %all_to_all.30.col_ref), channel_id=1, source_target_pairs={{0,8},{4,12},{8,0},{12,4},{1,9},{5,13},{9,1},{13,5},{2,10},{6,14},... | collective-permute-start | bytes 688136 | tf_op jit(solution)/shard_map/ppermute | solution.py:262
  48.6 0.0 copy-done.3
  48.6 5.0 %shard_map.52 = (f32[8,96,128]{2,1,0:T(8,128)S(1)}, f32[8,96,128]{2,1,0:T(8,128)S(1)}) custom-call(s32[1]{0:T(128)} %bitcast.core_ref, f32[3]{0:T(128)S(1)} %copy-done.3, bf16[16,16,128]{2,1,0:T(8,128)(2,1)S(1)} %all-to-all-done.row_ref, bf16[8,112,128]{2,1,0:T(8,128)(2,1)S(1)} %all_to_all.30.col_ref), custom_call_target="tpu_custom_call" | custom-call | flops 1610612736 | bytes 393216 | tf_op jit(solution)/shard_map/pallas_call | solution.py:73
  53.6 0.0 collective-permute-done.2.col_ref
  53.6 5.1 %shard_map.53 = (f32[8,96,128]{2,1,0:T(8,128)S(1)}, f32[8,96,128]{2,1,0:T(8,128)S(1)}) custom-call(s32[1]{0:T(128)} %bitcast.core_ref, f32[3]{0:T(128)S(1)} %copy-done.3, bf16[16,16,128]{2,1,0:T(8,128)(2,1)S(1)} %all-to-all-done.row_ref, bf16[8,112,128]{2,1,0:T(8,128)(2,1)S(1)} %collective-permute-done.2.col_ref, ...), custom_call_target="tpu_custom_call", output_to_operand_aliasing={{0}: (4, {}), {1}: (5, {})} | custom-call | flops 1610612736 | bytes 393216 | tf_op jit(solution)/shard_map/pallas_call | solution.py:73
  58.7 1.8 %collective-permute-done.1.col_ref = bf16[8,112,128]{2,1,0:T(8,128)(2,1)S(1)} collective-permute-done((bf16[8,112,128]{2,1,0:T(8,128)(2,1)S(1)}, bf16[8,112,128]{2,1,0:T(8,128)(2,1)S(1)}, u32[]{:S(2)}, u32[]{:S(2)}) %collective-permute-start.1) | collective-permute-done | bytes 229408 | tf_op jit(solution)/shard_map/ppermute | solution.py:262
  60.5 5.2 %shard_map.54 = (f32[8,96,128]{2,1,0:T(8,128)S(1)}, f32[8,96,128]{2,1,0:T(8,128)S(1)}) custom-call(s32[1]{0:T(128)} %bitcast.core_ref, f32[3]{0:T(128)S(1)} %copy-done.3, bf16[16,16,128]{2,1,0:T(8,128)(2,1)S(1)} %all-to-all-done.row_ref, bf16[8,112,128]{2,1,0:T(8,128)(2,1)S(1)} %collective-permute-done.1.col_ref, ...), custom_call_target="tpu_custom_call", output_to_operand_aliasing={{0}: (4, {}), {1}: (5, {})} | custom-call | flops 1610612736 | bytes 393216 | tf_op jit(solution)/shard_map/pallas_call | solution.py:73
  65.7 0.0 collective-permute-done.col_ref
  65.8 3.0 %shard_map.56 = f32[8,96,128]{2,1,0:T(8,128)S(1)} custom-call(s32[1]{0:T(128)} %bitcast.core_ref, f32[3]{0:T(128)S(1)} %copy-done.3, bf16[16,16,128]{2,1,0:T(8,128)(2,1)S(1)} %all-to-all-done.row_ref, bf16[8,112,128]{2,1,0:T(8,128)(2,1)S(1)} %collective-permute-done.col_ref, f32[8,96,128]{2,1,0:T(8,128)S(1)} %get-tuple-element.19.refs_0_), custom_call_target="tpu_custom_call", output_to_operand_aliasing={{}: (4, {})} | custom-call | flops 805306368 | bytes 393216 | tf_op jit(solution)/shard_map/pallas_call | solution.py:73
  68.8 3.0 %collective-permute-start.3 = (f32[8,96,128]{2,1,0:T(8,128)S(1)}, f32[8,96,128]{2,1,0:T(8,128)S(1)}, u32[]{:S(2)}, u32[]{:S(2)}) collective-permute-start(f32[8,96,128]{2,1,0:T(8,128)S(1)} %shard_map.56), channel_id=1, source_target_pairs={{0,1},{1,0},{2,3},{3,2},{4,5},{5,4},{6,7},{7,6},{8,9},{9,8},{10,11... | collective-permute-start | bytes 1179656 | tf_op jit(solution)/shard_map/ppermute | solution.py:269
  71.8 3.0 %shard_map.55 = f32[8,96,128]{2,1,0:T(8,128)S(1)} custom-call(s32[1]{0:T(128)} %bitcast.core_ref, f32[3]{0:T(128)S(1)} %copy-done.3, bf16[16,16,128]{2,1,0:T(8,128)(2,1)S(1)} %all-to-all-done.row_ref, bf16[8,112,128]{2,1,0:T(8,128)(2,1)S(1)} %collective-permute-done.col_ref, f32[8,96,128]{2,1,0:T(8,128)S(1)} %get-tuple-element.18.refs_0_), custom_call_target="tpu_custom_call", output_to_operand_aliasing={{}: (4, {})} | custom-call | flops 805306368 | bytes 393216 | tf_op jit(solution)/shard_map/pallas_call | solution.py:73
  74.8 0.0 collective-permute-done.3
  74.9 11.6 %all_to_all.31.part_ref = f32[8,96,128]{2,1,0:T(8,128)S(1)} all-to-all(f32[8,96,128]{2,1,0:T(8,128)S(1)} %add.3), channel_id=1, replica_groups=mesh['xh'=2,'xl'=2,'zh'=4,'zl'=2,'yh'=4,'yl'=2,'c'=2] {'xh','xl','yl'}, dimensions={0} | all-to-all | bytes 786432 | tf_op jit(solution)/shard_map/all_to_all | solution.py:271
  86.5 0.5 shard_map.57
  87.0 11.2 %all_to_all.32.part_ref = f32[32,8,128]{2,1,0:T(8,128)S(1)} all-to-all(f32[32,8,128]{2,1,0:T(8,128)S(1)} %get-tuple-element.20), channel_id=1, replica_groups=mesh['xh'=2,'xl'=2,'zh'=4,'zl'=2,'yh'=4,'yl'=2,'c'=2] {'xh','xl','zl','y..., dimensions={0} | all-to-all | bytes 262144 | tf_op jit(solution)/shard_map/all_to_all | solution.py:284
  98.2 22.0 %all_to_all.33.part_ref = f32[16,8,128]{2,1,0:T(8,128)S(1)} all-to-all(f32[16,8,128]{2,1,0:T(8,128)S(1)} %shard_map.58), channel_id=1, replica_groups=mesh['xh'=2,'xl'=2,'zh'=4,'zl'=2,'yh'=4,'yl'=2,'c'=2] {'zh','yh'}, dimensions={0} | all-to-all | bytes 131072 | tf_op jit(solution)/shard_map/all_to_all | solution.py:284
  120.3 11.7 %all_to_all.34.gram_ref = f32[32,8,128]{2,1,0:T(8,128)S(1)} all-to-all(f32[32,8,128]{2,1,0:T(8,128)S(1)} %shard_map.59), channel_id=1, replica_groups=mesh['xh'=2,'xl'=2,'zh'=4,'zl'=2,'yh'=4,'yl'=2,'c'=2] {'xh','xl','zl','y..., dimensions={0} | all-to-all | bytes 262144 | tf_op jit(solution)/shard_map/all_to_all | solution.py:286
  132.0 8.3 %shard_map.60 = (f32[96,128]{1,0:T(8,128)}, f32[96,96]{1,0:T(8,128)}) custom-call(f32[32,8,128]{2,1,0:T(8,128)S(1)} %all_to_all.34.gram_ref, f32[96,128]{1,0:T(8,128)S(1)} %get-tuple-element.21.image_ref), custom_call_target="tpu_custom_call" | custom-call | tf_op jit(solution)/shard_map/pallas_call | solution.py:243
  (4 shorter events, 0.1 us)
Async XLA Ops:
  0.6 0.7 copy-start.1
  1.9 10.3 %copy-start = (f32[96,128]{1,0:T(8,128)S(1)}, f32[96,128]{1,0:T(8,128)}, u32[]{:S(2)}) copy-start(f32[96,128]{1,0:T(8,128)} %mode_ref.3) | copy-start | bytes 147460
  1.9 10.3 %copy-start.2 = (s32[3,128]{1,0:T(4,128)S(1)}, s32[3,128]{1,0:T(4,128)}, u32[]{:S(2)}) copy-start(s32[3,128]{1,0:T(4,128)} %coord_ref.3) | copy-start | bytes 4612
  2.0 16.2 %all-to-all-start = ((bf16[16,16,128]{2,1,0:T(8,128)(2,1)}), bf16[16,16,128]{2,1,0:T(8,128)(2,1)S(1)}, u32[]{:S(2)}, u32[]{:S(2)}) async-start(bf16[16,16,128]{2,1,0:T(8,128)(2,1)} %shard_map.51), calls=%async_computation | async-start | bytes 131072 | tf_op jit(solution)/shard_map/all_to_all | solution.py:254
  34.6 19.0 %collective-permute-start.2 = (bf16[8,112,128]{2,1,0:T(8,128)(2,1)S(1)}, bf16[8,112,128]{2,1,0:T(8,128)(2,1)S(1)}, u32[]{:S(2)}, u32[]{:S(2)}) collective-permute-start(bf16[8,112,128]{2,1,0:T(8,128)(2,1)S(1)} %all_to_all.30.col_ref), channel_id=1, source_target_pairs={{0,4},{4,8},{8,12},{12,0},{1,5},{5,9},{9,13},{13,1},{2,6},{6,10},{... | collective-permute-start | bytes 688136 | tf_op jit(solution)/shard_map/ppermute | solution.py:262
  38.8 9.8 %copy-start.3 = (f32[3]{0:T(128)S(1)}, f32[3]{0:T(128)}, u32[]{:S(2)}) copy-start(f32[3]{0:T(128)} %range_ref.9) | copy-start | bytes 40
  38.9 21.6 %collective-permute-start.1 = (bf16[8,112,128]{2,1,0:T(8,128)(2,1)S(1)}, bf16[8,112,128]{2,1,0:T(8,128)(2,1)S(1)}, u32[]{:S(2)}, u32[]{:S(2)}) collective-permute-start(bf16[8,112,128]{2,1,0:T(8,128)(2,1)S(1)} %all_to_all.30.col_ref), channel_id=1, source_target_pairs={{0,12},{4,0},{8,4},{12,8},{1,13},{5,1},{9,5},{13,9},{2,14},{6,2},{... | collective-permute-start | bytes 688136 | tf_op jit(solution)/shard_map/ppermute | solution.py:262
  42.0 23.7 %collective-permute-start = (bf16[8,112,128]{2,1,0:T(8,128)(2,1)S(1)}, bf16[8,112,128]{2,1,0:T(8,128)(2,1)S(1)}, u32[]{:S(2)}, u32[]{:S(2)}) collective-permute-start(bf16[8,112,128]{2,1,0:T(8,128)(2,1)S(1)} %all_to_all.30.col_ref), channel_id=1, source_target_pairs={{0,8},{4,12},{8,0},{12,4},{1,9},{5,13},{9,1},{13,5},{2,10},{6,14},... | collective-permute-start | bytes 688136 | tf_op jit(solution)/shard_map/ppermute | solution.py:262
  68.8 6.1 %collective-permute-start.3 = (f32[8,96,128]{2,1,0:T(8,128)S(1)}, f32[8,96,128]{2,1,0:T(8,128)S(1)}, u32[]{:S(2)}, u32[]{:S(2)}) collective-permute-start(f32[8,96,128]{2,1,0:T(8,128)S(1)} %shard_map.56), channel_id=1, source_target_pairs={{0,1},{1,0},{2,3},{3,2},{4,5},{5,4},{6,7},{7,6},{8,9},{9,8},{10,11... | collective-permute-start | bytes 1179656 | tf_op jit(solution)/shard_map/ppermute | solution.py:269

commit v5 on v3

--- a/solution.py
+++ b/solution.py
@@ -10,14 +10,8 @@
 
 NUGGET = 0.25
 LOG2E = math.log2(math.e)
-CENTRE = 512.0
 HIGHEST = lax.Precision.HIGHEST
 PARAMS = pltpu.CompilerParams(vmem_limit_bytes=48 * 1024 * 1024)
-
-
-def scaled_coords(pack, scale):
-    parts = pack.astype(jnp.float32)
-    return (parts[0:8] * 4.0 + (parts[8:16] - CENTRE)) * scale
 
 
 def scale_rows(range_ref):
@@ -30,36 +24,57 @@
     return picked * LOG2E
 
 
+def split(pack, centre):
+    parts = pack.astype(jnp.float32)
+    return (parts[0:8] - centre) * 4.0, parts[8:16]
+
+
+def three_parts(value):
+    one = value.astype(jnp.bfloat16).astype(jnp.float32)
+    two = (value - one).astype(jnp.bfloat16).astype(jnp.float32)
+    return [one, two, value - one - two]
+
+
 def cov_kernel(halves, modes, core_ref, range_ref, row_ref, col_ref, *refs):
     count = len(halves)
     start_refs, refs = refs[: len(refs) - 2 - count], refs[len(refs) - 2 - count :]
     out_refs, (rows, cols) = refs[:count], refs[count:]
     pieces, _, width = col_ref.shape
     dests = row_ref.shape[0] // 2
-    scale = scale_rows(range_ref)
+    weight = scale_rows(range_ref)
+    weight = weight * weight
+    ones, blank = jnp.ones((1, width), jnp.float32), jnp.zeros((8, width), jnp.float32)
+    total = sum(row_ref[k, 0:8, :].astype(jnp.float32) for k in range(2 * dests))
+    centre = jnp.round(jnp.sum(total, axis=1, keepdims=True) * (1.0 / (2 * dests * width)))
     low = jnp.concatenate([col_ref[piece, 0:modes, :] for piece in range(pieces)], axis=1)
     for piece in range(pieces):
-        coords = scaled_coords(col_ref[piece, modes : modes + 16, :], scale).T
-        for d in range(3):
-            cols[d, piece * width : (piece + 1) * width, :] = jnp.broadcast_to(coords[:, d : d + 1], (width, width))
+        high, rest = split(col_ref[piece, modes : modes + 16, :], centre)
+        norm = jnp.sum(weight * (high + rest) * (high + rest), axis=0, keepdims=True)
+        norms = jnp.concatenate([ones] * 3 + three_parts(norm) + [blank[0:2]], axis=0)
+        features = jnp.concatenate([high] * 3 + [rest] * 3 + [norms, blank], axis=0)
+        cols[piece * width : (piece + 1) * width, :] = features.T.astype(jnp.bfloat16)
     for which, half in enumerate(halves):
         core = core_ref[0] if half == 0 else 1 - core_ref[0]
         for y in range(dests):
-            rows[which, :, y * width : (y + 1) * width] = scaled_coords(row_ref[2 * y + core], scale)
-        for pair in range(dests // 2):
-            parts = []
-            for y in (2 * pair, 2 * pair + 1):
-                total = LOG2E * LOG2E
-                for d in range(3):
-                    delta = cols[d] - rows[which, d : d + 1, y * width : (y + 1) * width]
-                    total = total + delta * delta
-                parts.append(jnp.exp2(LOG2E - total * lax.rsqrt(total)).astype(jnp.bfloat16))
-            update = jnp.dot(low, jnp.concatenate(parts, axis=1), preferred_element_type=jnp.float32)
-            for y in range(2):
+            high, rest = split(row_ref[2 * y + core], centre)
+            place = high + rest
+            norm = jnp.sum(weight * place * place, axis=0, keepdims=True) + LOG2E * LOG2E
+            norms = jnp.concatenate(three_parts(norm) + [ones] * 3 + [blank[0:2]], axis=0)
+            cross = three_parts(-2.0 * weight * place)
+            features = jnp.concatenate(cross + cross + [norms, blank], axis=0)
+            rows[which, :, y * width : (y + 1) * width] = features.astype(jnp.bfloat16)
+        group = 4
+        for first in range(0, dests, group):
+            span = slice(first * width, (first + group) * width)
+            total = jnp.dot(cols[...], rows[which, :, span], preferred_element_type=jnp.float32)
+            total = jnp.maximum(total, LOG2E * LOG2E)
+            cov = jnp.exp2(LOG2E - total * lax.rsqrt(total)).astype(jnp.bfloat16)
+            update = jnp.dot(low, cov, preferred_element_type=jnp.float32)
+            for y in range(group):
                 term = update[:, y * width : (y + 1) * width]
                 if start_refs:
-                    term = term + start_refs[which][2 * pair + y]
-                out_refs[which][2 * pair + y] = term
+                    term = term + start_refs[which][first + y]
+                out_refs[which][first + y] = term
 
 
 def covariance_part(core, inv_range, row_pack, col_pack, halves, starts=()):
@@ -76,8 +91,8 @@
         in_specs=[smem, smem] + [vmem] * (len(args) - 2),
         out_specs=[vmem] * len(halves),
         scratch_shapes=[
-            pltpu.VMEM((len(halves), 8, dests * width), jnp.float32),
-            pltpu.VMEM((3, col_pack.shape[0] * width, width), jnp.float32),
+            pltpu.VMEM((len(halves), 64, dests * width), jnp.bfloat16),
+            pltpu.VMEM((col_pack.shape[0] * width, 64), jnp.bfloat16),
         ],
         input_output_aliases={4 + k: k for k in range(len(starts))},
         compiler_params=PARAMS,

time: 135 us -> 133 us (0.985)
  Pallas kernels: 29.3 us -> 24.4 us
    pallas_call x3, Pallas kernels: 19.7 us -> 14.8 us  [covariance_part(): pl.pallas_call(functools.partial(cov_kernel, halves, modes), out_shape=[j...]
  transfers between devices with their start and end apart: 3 -> 3, of which waited for: 1 -> 2; matrix products, arithmetic and copies ran while one was open for 0% -> 0% of each run, Pallas kernels for 11% -> 8%
where the time goes in v5:
time: 133 us
  blocking collectives  80 us (60%)
  Pallas kernels  24.4 us (18%)
  starting transfers between devices  20.1 us (15%)
  waiting for transfers between devices  6.16 us (5%)
  local copies, waits for them, and re-layouts  1.33 us (1%)
    all_to_all x2, blocking collectives, body(): grams = lax.all_to_all(grams, axes, 0, 0)  30.1 us
    all_to_all x1, blocking collectives, body(): block = lax.all_to_all(block, far_axes, 0, 0)  27.1 us
    pallas_call x3, Pallas kernels, covariance_part(): pl.pallas_call(functools.partial(cov_kernel, halves, modes), out_shape=[j...  14.8 us
    all_to_all x1, blocking collectives, body(): grams = lax.all_to_all(grams, split_axes, 0, 0)  11.7 us
    all_to_all x1, blocking collectives, body(): pieces = lax.all_to_all(near + far, near_axes, 0, 0)  11 us
    all_to_all x1, starting transfers between devices, body(): row_pack = lax.all_to_all(row_pack, near_axes + ('c',), 0, 0)  10.3 us
    pallas_call x6, Pallas kernels, call(): pl.pallas_call(kernel, out_shape=out_shape, compiler_params=PARAMS)(*args)  9.58 us
    ppermute x1, starting transfers between devices, body(): far = lax.ppermute(far, 'c', [(0, 1), (1, 0)])  5.43 us
  transfers between devices with their start and end apart: 3, of which 2 were waited for; matrix products, arithmetic and copies ran while one was open for 0% of the time, Pallas kernels for 8%

profile of v5, /device:TPU:1, one launch (start us, length us, event | category | flops | bytes accessed | tf_op | source)
XLA Modules:
  0.0 132.7 jit_solution(3301827478908027159)
XLA Ops:
  0.6 0.0 copy-start.1
  0.6 0.7 copy-done.1
  1.3 0.6 shard_map.51
  1.9 0.0 copy-start
  1.9 0.0 copy-start.2
  1.9 10.3 %all-to-all-start = ((bf16[16,16,128]{2,1,0:T(8,128)(2,1)}), bf16[16,16,128]{2,1,0:T(8,128)(2,1)S(1)}, u32[]{:S(2)}, u32[]{:S(2)}) async-start(bf16[16,16,128]{2,1,0:T(8,128)(2,1)} %shard_map.51), calls=%async_computation | async-start | bytes 131072 | tf_op jit(solution)/shard_map/all_to_all | solution.py:268
  12.2 0.0 copy-done
  12.2 0.0 copy-done.2
  12.3 5.1 %all-to-all-done.row_ref = bf16[16,16,128]{2,1,0:T(8,128)(2,1)S(1)} async-done(((bf16[16,16,128]{2,1,0:T(8,128)(2,1)}), bf16[16,16,128]{2,1,0:T(8,128)(2,1)S(1)}, u32[]{:S(2)}, u32[]{:S(2)}) %all-to-all-start) | async-done | bytes 65568 | tf_op jit(solution)/shard_map/all_to_all | solution.py:268
  17.4 27.1 %all_to_all.30.col_ref = bf16[16,112,128]{2,1,0:T(8,128)(2,1)S(1)} all-to-all(bf16[16,112,128]{2,1,0:T(8,128)(2,1)S(1)} %shard_map.50), channel_id=1, replica_groups=mesh['xh'=2,'xl'=2,'zh'=4,'zl'=2,'yh'=4,'yl'=2,'c'=2] {'zh','yh'}, dimensions={0} | all-to-all | bytes 917504 | tf_op jit(solution)/shard_map/all_to_all | solution.py:273
  44.5 4.3 %collective-permute-start = (bf16[16,112,128]{2,1,0:T(8,128)(2,1)S(1)}, bf16[16,112,128]{2,1,0:T(8,128)(2,1)S(1)}, u32[]{:S(2)}, u32[]{:S(2)}) collective-permute-start(bf16[16,112,128]{2,1,0:T(8,128)(2,1)S(1)} %all_to_all.30.col_ref), channel_id=1, source_target_pairs={{0,256},{256,0},{1,257},{257,1},{2,258},{258,2},{3,259},{259,3},{4... | collective-permute-start | bytes 1376264 | tf_op jit(solution)/shard_map/ppermute | solution.py:274
  48.9 0.0 copy-start.3
  48.9 0.6 copy-done.3
  49.5 6.9 %shard_map.52 = (f32[8,96,128]{2,1,0:T(8,128)S(1)}, f32[8,96,128]{2,1,0:T(8,128)S(1)}) custom-call(s32[1]{0:T(128)} %bitcast.core_ref, f32[3]{0:T(128)S(1)} %copy-done.3, bf16[16,16,128]{2,1,0:T(8,128)(2,1)S(1)} %all-to-all-done.row_ref, bf16[16,112,128]{2,1,0:T(8,128)(2,1)S(1)} %all_to_all.30.col_ref), custom_call_target="tpu_custom_call" | custom-call | flops 3221225472 | bytes 393216 | tf_op jit(solution)/shard_map/pallas_call | solution.py:88
  56.4 1.1 collective-permute-done.col_ref
  57.5 3.9 %shard_map.54 = f32[8,96,128]{2,1,0:T(8,128)S(1)} custom-call(s32[1]{0:T(128)} %bitcast.core_ref, f32[3]{0:T(128)S(1)} %copy-done.3, bf16[16,16,128]{2,1,0:T(8,128)(2,1)S(1)} %all-to-all-done.row_ref, bf16[16,112,128]{2,1,0:T(8,128)(2,1)S(1)} %collective-permute-done.col_ref, f32[8,96,128]{2,1,0:T(8,128)S(1)} %get-tuple-element.11.refs_0_), custom_call_target="tpu_custom_call", output_to_operand_aliasing={{}: (4, {})} | custom-call | flops 1610612736 | bytes 393216 | tf_op jit(solution)/shard_map/pallas_call | solution.py:88
  61.4 5.4 %collective-permute-start.1 = (f32[8,96,128]{2,1,0:T(8,128)S(1)}, f32[8,96,128]{2,1,0:T(8,128)S(1)}, u32[]{:S(2)}, u32[]{:S(2)}) collective-permute-start(f32[8,96,128]{2,1,0:T(8,128)S(1)} %shard_map.54), channel_id=1, source_target_pairs={{0,1},{1,0},{2,3},{3,2},{4,5},{5,4},{6,7},{7,6},{8,9},{9,8},{10,11... | collective-permute-start | bytes 1179656 | tf_op jit(solution)/shard_map/ppermute | solution.py:279
  66.9 4.0 %shard_map.53 = f32[8,96,128]{2,1,0:T(8,128)S(1)} custom-call(s32[1]{0:T(128)} %bitcast.core_ref, f32[3]{0:T(128)S(1)} %copy-done.3, bf16[16,16,128]{2,1,0:T(8,128)(2,1)S(1)} %all-to-all-done.row_ref, bf16[16,112,128]{2,1,0:T(8,128)(2,1)S(1)} %collective-permute-done.col_ref, f32[8,96,128]{2,1,0:T(8,128)S(1)} %get-tuple-element.10.refs_0_), custom_call_target="tpu_custom_call", output_to_operand_aliasing={{}: (4, {})} | custom-call | flops 1610612736 | bytes 393216 | tf_op jit(solution)/shard_map/pallas_call | solution.py:88
  70.9 0.0 collective-permute-done.1
  70.9 0.1 add.3
  70.9 11.0 %all_to_all.31.part_ref = f32[8,96,128]{2,1,0:T(8,128)S(1)} all-to-all(f32[8,96,128]{2,1,0:T(8,128)S(1)} %add.3), channel_id=1, replica_groups=mesh['xh'=2,'xl'=2,'zh'=4,'zl'=2,'yh'=4,'yl'=2,'c'=2] {'xl','zl','yl'}, dimensions={0} | all-to-all | bytes 786432 | tf_op jit(solution)/shard_map/all_to_all | solution.py:281
  81.9 0.5 shard_map.55
  82.4 12.3 %all_to_all.32.part_ref = f32[32,8,128]{2,1,0:T(8,128)S(1)} all-to-all(f32[32,8,128]{2,1,0:T(8,128)S(1)} %get-tuple-element.12), channel_id=1, replica_groups=mesh['xh'=2,'xl'=2,'zh'=4,'zl'=2,'yh'=4,'yl'=2,'c'=2] {'xh','xl','zl','y..., dimensions={0} | all-to-all | bytes 262144 | tf_op jit(solution)/shard_map/all_to_all | solution.py:295
  94.7 17.9 %all_to_all.33.part_ref = f32[16,8,128]{2,1,0:T(8,128)S(1)} all-to-all(f32[16,8,128]{2,1,0:T(8,128)S(1)} %shard_map.56), channel_id=1, replica_groups=mesh['xh'=2,'xl'=2,'zh'=4,'zl'=2,'yh'=4,'yl'=2,'c'=2] {'zh','yh'}, dimensions={0} | all-to-all | bytes 131072 | tf_op jit(solution)/shard_map/all_to_all | solution.py:295
  112.6 11.7 %all_to_all.34.gram_ref = f32[32,8,128]{2,1,0:T(8,128)S(1)} all-to-all(f32[32,8,128]{2,1,0:T(8,128)S(1)} %shard_map.57), channel_id=1, replica_groups=mesh['xh'=2,'xl'=2,'zh'=4,'zl'=2,'yh'=4,'yl'=2,'c'=2] {'xh','xl','zl','y..., dimensions={0} | all-to-all | bytes 262144 | tf_op jit(solution)/shard_map/all_to_all | solution.py:297
  124.3 8.4 %shard_map.58 = (f32[96,128]{1,0:T(8,128)}, f32[96,96]{1,0:T(8,128)}) custom-call(f32[32,8,128]{2,1,0:T(8,128)S(1)} %all_to_all.34.gram_ref, f32[96,128]{1,0:T(8,128)S(1)} %get-tuple-element.13.image_ref), custom_call_target="tpu_custom_call" | custom-call | tf_op jit(solution)/shard_map/pallas_call | solution.py:258
  (3 shorter events, 0.1 us)
Async XLA Ops:
  0.6 0.7 copy-start.1
  1.9 10.3 %copy-start = (f32[96,128]{1,0:T(8,128)S(1)}, f32[96,128]{1,0:T(8,128)}, u32[]{:S(2)}) copy-start(f32[96,128]{1,0:T(8,128)} %mode_ref.3) | copy-start | bytes 147460
  1.9 10.3 %copy-start.2 = (s32[3,128]{1,0:T(4,128)S(1)}, s32[3,128]{1,0:T(4,128)}, u32[]{:S(2)}) copy-start(s32[3,128]{1,0:T(4,128)} %coord_ref.3) | copy-start | bytes 4612
  1.9 15.4 %all-to-all-start = ((bf16[16,16,128]{2,1,0:T(8,128)(2,1)}), bf16[16,16,128]{2,1,0:T(8,128)(2,1)S(1)}, u32[]{:S(2)}, u32[]{:S(2)}) async-start(bf16[16,16,128]{2,1,0:T(8,128)(2,1)} %shard_map.51), calls=%async_computation | async-start | bytes 131072 | tf_op jit(solution)/shard_map/all_to_all | solution.py:268
  44.5 13.0 %collective-permute-start = (bf16[16,112,128]{2,1,0:T(8,128)(2,1)S(1)}, bf16[16,112,128]{2,1,0:T(8,128)(2,1)S(1)}, u32[]{:S(2)}, u32[]{:S(2)}) collective-permute-start(bf16[16,112,128]{2,1,0:T(8,128)(2,1)S(1)} %all_to_all.30.col_ref), channel_id=1, source_target_pairs={{0,256},{256,0},{1,257},{257,1},{2,258},{258,2},{3,259},{259,3},{4... | collective-permute-start | bytes 1376264 | tf_op jit(solution)/shard_map/ppermute | solution.py:274
  48.9 0.7 copy-start.3
  61.4 9.4 %collective-permute-start.1 = (f32[8,96,128]{2,1,0:T(8,128)S(1)}, f32[8,96,128]{2,1,0:T(8,128)S(1)}, u32[]{:S(2)}, u32[]{:S(2)}) collective-permute-start(f32[8,96,128]{2,1,0:T(8,128)S(1)} %shard_map.54), channel_id=1, source_target_pairs={{0,1},{1,0},{2,3},{3,2},{4,5},{5,4},{6,7},{7,6},{8,9},{9,8},{10,11... | collective-permute-start | bytes 1179656 | tf_op jit(solution)/shard_map/ppermute | solution.py:279

commit v6 on v5

--- a/solution.py
+++ b/solution.py
@@ -35,14 +35,13 @@
     return [one, two, value - one - two]
 
 
-def cov_kernel(halves, modes, core_ref, range_ref, row_ref, col_ref, *refs):
+def cov_kernel(halves, modes, core_ref, weight_ref, row_ref, col_ref, *refs):
     count = len(halves)
     start_refs, refs = refs[: len(refs) - 2 - count], refs[len(refs) - 2 - count :]
     out_refs, (rows, cols) = refs[:count], refs[count:]
     pieces, _, width = col_ref.shape
     dests = row_ref.shape[0] // 2
-    weight = scale_rows(range_ref)
-    weight = weight * weight
+    weight = weight_ref[...]
     ones, blank = jnp.ones((1, width), jnp.float32), jnp.zeros((8, width), jnp.float32)
     total = sum(row_ref[k, 0:8, :].astype(jnp.float32) for k in range(2 * dests))
     centre = jnp.round(jnp.sum(total, axis=1, keepdims=True) * (1.0 / (2 * dests * width)))
@@ -77,18 +76,18 @@
                 out_refs[which][first + y] = term
 
 
-def covariance_part(core, inv_range, row_pack, col_pack, halves, starts=()):
+def covariance_part(core, weight, row_pack, col_pack, halves, starts=()):
     dests, _, width = row_pack.shape
     dests = dests // 2
     modes = col_pack.shape[1] - 16
     pairs = col_pack.shape[0] * dests * width * width * len(halves)
     vmem = pl.BlockSpec(memory_space=pltpu.VMEM)
     smem = pl.BlockSpec(memory_space=pltpu.SMEM)
-    args = (core, inv_range, row_pack, col_pack) + tuple(starts)
+    args = (core, weight, row_pack, col_pack) + tuple(starts)
     return pl.pallas_call(
         functools.partial(cov_kernel, halves, modes),
         out_shape=[jax.ShapeDtypeStruct((dests, modes, width), jnp.float32)] * len(halves),
-        in_specs=[smem, smem] + [vmem] * (len(args) - 2),
+        in_specs=[smem] + [vmem] * (len(args) - 1),
         out_specs=[vmem] * len(halves),
         scratch_shapes=[
             pltpu.VMEM((len(halves), 64, dests * width), jnp.bfloat16),
@@ -108,21 +107,19 @@
     )
 
 
-def pack_coords(coord_ref):
+def row_kernel(coord_ref, out_ref):
     coords = coord_ref[...].astype(jnp.float32)
     high = jnp.floor(coords * 0.25)
     blank = jnp.zeros((5, coords.shape[1]), jnp.float32)
-    return jnp.concatenate([high, blank, coords - 4.0 * high, blank], axis=0).astype(jnp.bfloat16)
-
-
-def row_kernel(coord_ref, out_ref):
-    pack = pack_coords(coord_ref)
+    pack = jnp.concatenate([high, blank, coords - 4.0 * high, blank], axis=0).astype(jnp.bfloat16)
     for k in range(out_ref.shape[0]):
         out_ref[k] = pack
 
 
-def block_kernel(coord_ref, mode_ref, out_ref):
-    pack = jnp.concatenate([mode_ref[...].astype(jnp.bfloat16), pack_coords(coord_ref)], axis=0)
+def block_kernel(range_ref, row_ref, mode_ref, out_ref, weight_ref):
+    scale = scale_rows(range_ref)
+    weight_ref[...] = scale * scale
+    pack = jnp.concatenate([mode_ref[...].astype(jnp.bfloat16), row_ref[0]], axis=0)
     for k in range(out_ref.shape[0]):
         out_ref[k] = pack
 
@@ -217,35 +214,48 @@
         return jnp.broadcast_to(value[:, k : k + 1], (8, width))
 
     done = [[None] * tiles, [None] * tiles]
-    for k in range(0, modes, 2):
+    for k in range(0, modes, 4):
         home, sub = divmod(k, 8)
-        near = [(spread_lane(left[m][home], k), spread_lane(left[m][home], k + 1)) for m in range(2)]
+        near = [[spread_lane(left[m][home], k + j) for j in range(4)] for m in range(2)]
         steps = []
         for m in range(2):
-            first, second = near[m]
-            p, q, r = spread_row(first, sub), spread_row(first, sub + 1), spread_row(second, sub + 1)
-            a0, a1 = spread_row(left[m][home], sub), spread_row(left[m][home], sub + 1)
-            b0, b1 = spread_row(right[m][home], sub), spread_row(right[m][home], sub + 1)
-            scale = 1.0 / (p * r - q * q)
-            steps.append(
-                ((r * a0 - q * a1) * scale, (p * a1 - q * a0) * scale, (r * b0 - q * b1) * scale, (p * b1 - q * b0) * scale)
+            e = {(i, j): spread_row(near[m][j], sub + i) for j in range(4) for i in range(j, 4)}
+            scale = 1.0 / (e[0, 0] * e[1, 1] - e[1, 0] * e[1, 0])
+            r, q, p = e[1, 1] * scale, e[1, 0] * scale, e[0, 0] * scale
+            u2, v2 = r * e[2, 0] - q * e[2, 1], p * e[2, 1] - q * e[2, 0]
+            u3, v3 = r * e[3, 0] - q * e[3, 1], p * e[3, 1] - q * e[3, 0]
+            s22 = e[2, 2] - (e[2, 0] * u2 + e[2, 1] * v2)
+            s32 = e[3, 2] - (e[3, 0] * u2 + e[3, 1] * v2)
+            s33 = e[3, 3] - (e[3, 0] * u3 + e[3, 1] * v3)
+            scale = 1.0 / (s22 * s33 - s32 * s32)
+            rr, qq, pp = s33 * scale, s32 * scale, s22 * scale
+            found = []
+            for value in (left[m][home], right[m][home]):
+                g0, g1, g2, g3 = (spread_row(value, sub + i) for i in range(4))
+                h2, h3 = g2 - (u2 * g0 + v2 * g1), g3 - (u3 * g0 + v3 * g1)
+                x2, x3 = rr * h2 - qq * h3, pp * h3 - qq * h2
+                x0 = (r * g0 - q * g1) - (u2 * x2 + u3 * x3)
+                x1 = (p * g1 - q * g0) - (v2 * x2 + v3 * x3)
+                found.append((x0, x1, x2, x3))
+            steps.append(found)
+            flat, flat2 = 1.0 / e[0, 0], 1.0 / s22
+            ratio, ratio2 = e[1, 0] * flat, s32 * flat2
+            y0, y1 = g0 * jnp.sqrt(flat), (g1 - ratio * g0) / jnp.sqrt(e[1, 1] - ratio * e[1, 0])
+            y2, y3 = h2 * jnp.sqrt(flat2), (h3 - ratio2 * h2) / jnp.sqrt(s33 - ratio2 * s32)
+            rows = jnp.where(
+                row < sub + 2, jnp.where(row == sub, y0, y1), jnp.where(row == sub + 2, y2, y3)
             )
-            flat = 1.0 / p
-            ratio = q * flat
-            rows = jnp.where(row == sub, b0 * jnp.sqrt(flat), (b1 - ratio * b0) / jnp.sqrt(r - ratio * q))
             done[m][home] = rows if sub == 0 else jnp.where(row >= sub, rows, done[m][home])
         for t in range(home, tiles):
             for m in range(2):
-                a, b = left[m], right[m]
                 if t > home:
-                    f0, f1 = spread_lane(a[t], k), spread_lane(a[t], k + 1)
-                elif sub < 6:
-                    f0, f1 = (jnp.where(row > sub + 1, part, 0.0) for part in near[m])
+                    f = [spread_lane(left[m][t], k + j) for j in range(4)]
+                elif sub == 0:
+                    f = [jnp.where(row > 3, part, 0.0) for part in near[m]]
                 else:
                     continue
-                a0, a1, b0, b1 = steps[m]
-                a[t] = a[t] - (f0 * a0 + f1 * a1)
-                b[t] = b[t] - (f0 * b0 + f1 * b1)
+                for side, x in zip((left[m], right[m]), steps[m]):
+                    side[t] = side[t] - ((f[0] * x[0] + f[1] * x[1]) + (f[2] * x[2] + f[3] * x[3]))
 
     basis_ref[...] = jnp.concatenate(done[0], axis=0)
     inverse = jnp.concatenate(done[1], axis=0)[:, 0:modes]
@@ -264,16 +274,23 @@
     count = {axis: lax.axis_size(axis) for axis in near_axes + far_axes + (last, "c")}
     dests, sources = (math.prod(count[axis] for axis in axes) for axes in (near_axes, far_axes))
     node_total = math.prod(count.values()) * width
-    row_pack = call(row_kernel, jax.ShapeDtypeStruct((2 * dests, 16, width), jnp.bfloat16), node_coords)
-    row_pack = lax.all_to_all(row_pack, near_axes + ("c",), 0, 0)
-    block = call(
-        block_kernel, jax.ShapeDtypeStruct((sources, modes + 16, width), jnp.bfloat16), node_coords, mode_block
-    )
+    row_send = call(row_kernel, jax.ShapeDtypeStruct((2 * dests, 16, width), jnp.bfloat16), node_coords)
+    row_pack = lax.all_to_all(row_send, near_axes + ("c",), 0, 0)
+    vmem = pl.BlockSpec(memory_space=pltpu.VMEM)
+    block, weight = pl.pallas_call(
+        block_kernel,
+        out_shape=(
+            jax.ShapeDtypeStruct((sources, modes + 16, width), jnp.bfloat16),
+            jax.ShapeDtypeStruct((8, width), jnp.float32),
+        ),
+        in_specs=[pl.BlockSpec(memory_space=pltpu.SMEM), vmem, vmem],
+        compiler_params=PARAMS,
+    )(inv_range, row_send, mode_block)
     block, row_pack = lax.optimization_barrier((block, row_pack))
     block = lax.all_to_all(block, far_axes, 0, 0)
     other = lax.ppermute(block, last, [(0, 1), (1, 0)])
     core = lax.axis_index("c").astype(jnp.int32)[None]
-    shared = functools.partial(covariance_part, core, inv_range, row_pack)
+    shared = functools.partial(covariance_part, core, weight, row_pack)
     far, near = shared(block, (1, 0))
     (far,) = shared(other, (1,), (far,))
     far = lax.ppermute(far, "c", [(0, 1), (1, 0)])

time: 133 us -> 130 us (0.977)
  Pallas kernels: 24.4 us -> 21.4 us
    pallas_call x6 -> x5, Pallas kernels: 9.58 us -> 7.36 us  [call(): pl.pallas_call(kernel, out_shape=out_shape, compiler_params=PARAMS)(*args)]
    pallas_call x3, Pallas kernels: 14.8 us -> 13.2 us  [covariance_part(): pl.pallas_call(functools.partial(cov_kernel, halves, modes), out_shape=[j...]
where the time goes in v6:
time: 130 us; the launch traced here: 129 us
  blocking collectives  80 us (62%)
  Pallas kernels  21.4 us (16%)
  starting transfers between devices  20.1 us (15%)
  waiting for transfers between devices  6.51 us (5%)
    all_to_all x2, blocking collectives, body(): grams = lax.all_to_all(grams, axes, 0, 0)  30.2 us
    all_to_all x1, blocking collectives, body(): block = lax.all_to_all(block, far_axes, 0, 0)  27.1 us
    pallas_call x3, Pallas kernels, covariance_part(): pl.pallas_call(functools.partial(cov_kernel, halves, modes), out_shape=[j...  13.2 us
    all_to_all x1, blocking collectives, body(): grams = lax.all_to_all(grams, split_axes, 0, 0)  11.7 us
    all_to_all x1, blocking collectives, body(): pieces = lax.all_to_all(near + far, near_axes, 0, 0)  10.9 us
    all_to_all x1, starting transfers between devices, body(): row_pack = lax.all_to_all(row_send, near_axes + ('c',), 0, 0)  10.3 us
    pallas_call x5, Pallas kernels, call(): pl.pallas_call(kernel, out_shape=out_shape, compiler_params=PARAMS)(*args)  7.36 us
    ppermute x1, starting transfers between devices, body(): far = lax.ppermute(far, 'c', [(0, 1), (1, 0)])  5.45 us
  transfers between devices with their start and end apart: 3, of which 2 were waited for; matrix products, arithmetic and copies ran while one was open for 0% of the time, Pallas kernels for 8%

profile of v6, /device:TPU:1, one launch (start us, length us, event | category | flops | bytes accessed | tf_op | source)
XLA Modules:
  0.0 129.4 jit_solution(10038288195713015171)
XLA Ops:
  0.6 0.0 copy-start.1
  0.6 0.7 copy-done.1
  1.3 0.6 shard_map.50.row_ref
  1.9 0.0 copy-start
  1.9 0.0 copy-start.2
  1.9 10.3 %all-to-all-start = ((bf16[16,16,128]{2,1,0:T(8,128)(2,1)}), bf16[16,16,128]{2,1,0:T(8,128)(2,1)S(1)}, u32[]{:S(2)}, u32[]{:S(2)}) async-start(bf16[16,16,128]{2,1,0:T(8,128)(2,1)} %shard_map.50.row_ref), calls=%async_computation | async-start | bytes 131072 | tf_op jit(solution)/shard_map/all_to_all | solution.py:278
  12.2 0.0 copy-done
  12.2 0.0 copy-done.2
  12.2 0.9 shard_map.51
  13.2 4.2 %all-to-all-done.row_ref = bf16[16,16,128]{2,1,0:T(8,128)(2,1)S(1)} async-done(((bf16[16,16,128]{2,1,0:T(8,128)(2,1)}), bf16[16,16,128]{2,1,0:T(8,128)(2,1)S(1)}, u32[]{:S(2)}, u32[]{:S(2)}) %all-to-all-start) | async-done | bytes 65568 | tf_op jit(solution)/shard_map/all_to_all | solution.py:278
  17.4 27.1 %all_to_all.30.col_ref = bf16[16,112,128]{2,1,0:T(8,128)(2,1)S(1)} all-to-all(bf16[16,112,128]{2,1,0:T(8,128)(2,1)S(1)} %get-tuple-element.13), channel_id=1, replica_groups=mesh['xh'=2,'xl'=2,'zh'=4,'zl'=2,'yh'=4,'yl'=2,'c'=2] {'zh','yh'}, dimensions={0} | all-to-all | bytes 917504 | tf_op jit(solution)/shard_map/all_to_all | solution.py:290
  44.5 4.3 %collective-permute-start = (bf16[16,112,128]{2,1,0:T(8,128)(2,1)S(1)}, bf16[16,112,128]{2,1,0:T(8,128)(2,1)S(1)}, u32[]{:S(2)}, u32[]{:S(2)}) collective-permute-start(bf16[16,112,128]{2,1,0:T(8,128)(2,1)S(1)} %all_to_all.30.col_ref), channel_id=1, source_target_pairs={{0,256},{256,0},{1,257},{257,1},{2,258},{258,2},{3,259},{259,3},{4... | collective-permute-start | bytes 1376264 | tf_op jit(solution)/shard_map/ppermute | solution.py:291
  48.9 6.3 %shard_map.52 = (f32[8,96,128]{2,1,0:T(8,128)S(1)}, f32[8,96,128]{2,1,0:T(8,128)S(1)}) custom-call(s32[1]{0:T(128)} %bitcast.core_ref, f32[8,128]{1,0:T(8,128)S(1)} %get-tuple-element.10.weight_ref, bf16[16,16,128]{2,1,0:T(8,128)(2,1)S(1)} %all-to-all-done.row_ref, bf16[16,112,128]{2,1,0:T(8,128)(2,1)S(1)} %all_to_all.30.col_ref), custom_call_target="tpu_custom_call" | custom-call | flops 3221225472 | bytes 393216 | tf_op jit(solution)/shard_map/pallas_call | solution.py:87
  55.2 2.3 %collective-permute-done.col_ref = bf16[16,112,128]{2,1,0:T(8,128)(2,1)S(1)} collective-permute-done((bf16[16,112,128]{2,1,0:T(8,128)(2,1)S(1)}, bf16[16,112,128]{2,1,0:T(8,128)(2,1)S(1)}, u32[]{:S(2)}, u32[]{:S(2)}) %collective-permute-start) | collective-permute-done | bytes 458784 | tf_op jit(solution)/shard_map/ppermute | solution.py:291
  57.5 3.4 %shard_map.54 = f32[8,96,128]{2,1,0:T(8,128)S(1)} custom-call(s32[1]{0:T(128)} %bitcast.core_ref, f32[8,128]{1,0:T(8,128)S(1)} %get-tuple-element.10.weight_ref, bf16[16,16,128]{2,1,0:T(8,128)(2,1)S(1)} %all-to-all-done.row_ref, bf16[16,112,128]{2,1,0:T(8,128)(2,1)S(1)} %collective-permute-done.col_ref, ...), custom_call_target="tpu_custom_call", output_to_operand_aliasing={{}: (4, {})} | custom-call | flops 1610612736 | bytes 393216 | tf_op jit(solution)/shard_map/pallas_call | solution.py:87
  60.9 5.4 %collective-permute-start.1 = (f32[8,96,128]{2,1,0:T(8,128)S(1)}, f32[8,96,128]{2,1,0:T(8,128)S(1)}, u32[]{:S(2)}, u32[]{:S(2)}) collective-permute-start(f32[8,96,128]{2,1,0:T(8,128)S(1)} %shard_map.54), channel_id=1, source_target_pairs={{0,1},{1,0},{2,3},{3,2},{4,5},{5,4},{6,7},{7,6},{8,9},{9,8},{10,11... | collective-permute-start | bytes 1179656 | tf_op jit(solution)/shard_map/ppermute | solution.py:296
  66.4 3.4 %shard_map.53 = f32[8,96,128]{2,1,0:T(8,128)S(1)} custom-call(s32[1]{0:T(128)} %bitcast.core_ref, f32[8,128]{1,0:T(8,128)S(1)} %get-tuple-element.10.weight_ref, bf16[16,16,128]{2,1,0:T(8,128)(2,1)S(1)} %all-to-all-done.row_ref, bf16[16,112,128]{2,1,0:T(8,128)(2,1)S(1)} %collective-permute-done.col_ref, ...), custom_call_target="tpu_custom_call", output_to_operand_aliasing={{}: (4, {})} | custom-call | flops 1610612736 | bytes 393216 | tf_op jit(solution)/shard_map/pallas_call | solution.py:87
  69.8 0.0 collective-permute-done.1
  69.9 10.9 %all_to_all.31.part_ref = f32[8,96,128]{2,1,0:T(8,128)S(1)} all-to-all(f32[8,96,128]{2,1,0:T(8,128)S(1)} %add.3), channel_id=1, replica_groups=mesh['xh'=2,'xl'=2,'zh'=4,'zl'=2,'yh'=4,'yl'=2,'c'=2] {'xl','zl','yl'}, dimensions={0} | all-to-all | bytes 786432 | tf_op jit(solution)/shard_map/all_to_all | solution.py:298
  80.8 0.5 shard_map.55
  81.3 12.3 %all_to_all.32.part_ref = f32[32,8,128]{2,1,0:T(8,128)S(1)} all-to-all(f32[32,8,128]{2,1,0:T(8,128)S(1)} %get-tuple-element.16), channel_id=1, replica_groups=mesh['xh'=2,'xl'=2,'zh'=4,'zl'=2,'yh'=4,'yl'=2,'c'=2] {'xh','xl','zl','y..., dimensions={0} | all-to-all | bytes 262144 | tf_op jit(solution)/shard_map/all_to_all | solution.py:312
  93.6 17.9 %all_to_all.33.part_ref = f32[16,8,128]{2,1,0:T(8,128)S(1)} all-to-all(f32[16,8,128]{2,1,0:T(8,128)S(1)} %shard_map.56), channel_id=1, replica_groups=mesh['xh'=2,'xl'=2,'zh'=4,'zl'=2,'yh'=4,'yl'=2,'c'=2] {'zh','yh'}, dimensions={0} | all-to-all | bytes 131072 | tf_op jit(solution)/shard_map/all_to_all | solution.py:312
  111.5 11.7 %all_to_all.34.gram_ref = f32[32,8,128]{2,1,0:T(8,128)S(1)} all-to-all(f32[32,8,128]{2,1,0:T(8,128)S(1)} %shard_map.57), channel_id=1, replica_groups=mesh['xh'=2,'xl'=2,'zh'=4,'zl'=2,'yh'=4,'yl'=2,'c'=2] {'xh','xl','zl','y..., dimensions={0} | all-to-all | bytes 262144 | tf_op jit(solution)/shard_map/all_to_all | solution.py:314
  123.3 6.2 %shard_map.58 = (f32[96,128]{1,0:T(8,128)}, f32[96,96]{1,0:T(8,128)}) custom-call(f32[32,8,128]{2,1,0:T(8,128)S(1)} %all_to_all.34.gram_ref, f32[96,128]{1,0:T(8,128)S(1)} %get-tuple-element.17.image_ref), custom_call_target="tpu_custom_call" | custom-call | tf_op jit(solution)/shard_map/pallas_call | solution.py:268
  (3 shorter events, 0.1 us)
Async XLA Ops:
  0.6 0.7 copy-start.1
  1.9 10.3 %copy-start = (f32[96,128]{1,0:T(8,128)S(1)}, f32[96,128]{1,0:T(8,128)}, u32[]{:S(2)}) copy-start(f32[96,128]{1,0:T(8,128)} %mode_ref.3) | copy-start | bytes 147460
  1.9 10.3 %copy-start.2 = (f32[3]{0:T(128)S(1)}, f32[3]{0:T(128)}, u32[]{:S(2)}) copy-start(f32[3]{0:T(128)} %range_ref.1) | copy-start | bytes 40
  1.9 15.4 %all-to-all-start = ((bf16[16,16,128]{2,1,0:T(8,128)(2,1)}), bf16[16,16,128]{2,1,0:T(8,128)(2,1)S(1)}, u32[]{:S(2)}, u32[]{:S(2)}) async-start(bf16[16,16,128]{2,1,0:T(8,128)(2,1)} %shard_map.50.row_ref), calls=%async_computation | async-start | bytes 131072 | tf_op jit(solution)/shard_map/all_to_all | solution.py:278
  44.5 13.0 %collective-permute-start = (bf16[16,112,128]{2,1,0:T(8,128)(2,1)S(1)}, bf16[16,112,128]{2,1,0:T(8,128)(2,1)S(1)}, u32[]{:S(2)}, u32[]{:S(2)}) collective-permute-start(bf16[16,112,128]{2,1,0:T(8,128)(2,1)S(1)} %all_to_all.30.col_ref), channel_id=1, source_target_pairs={{0,256},{256,0},{1,257},{257,1},{2,258},{258,2},{3,259},{259,3},{4... | collective-permute-start | bytes 1376264 | tf_op jit(solution)/shard_map/ppermute | solution.py:291
  60.9 8.9 %collective-permute-start.1 = (f32[8,96,128]{2,1,0:T(8,128)S(1)}, f32[8,96,128]{2,1,0:T(8,128)S(1)}, u32[]{:S(2)}, u32[]{:S(2)}) collective-permute-start(f32[8,96,128]{2,1,0:T(8,128)S(1)} %shard_map.54), channel_id=1, source_target_pairs={{0,1},{1,0},{2,3},{3,2},{4,5},{5,4},{6,7},{7,6},{8,9},{9,8},{10,11... | collective-permute-start | bytes 1179656 | tf_op jit(solution)/shard_map/ppermute | solution.py:296

commit v7 on v6

--- a/solution.py
+++ b/solution.py
@@ -27,6 +27,14 @@
 def split(pack, centre):
     parts = pack.astype(jnp.float32)
     return (parts[0:8] - centre) * 4.0, parts[8:16]
+
+
+def halves_of(coords):
+    coords = coords.astype(jnp.float32)
+    if coords.shape[0] < 8:
+        coords = jnp.concatenate([coords, jnp.zeros((8 - coords.shape[0], coords.shape[1]), jnp.float32)], axis=0)
+    high = jnp.floor(coords * 0.25)
+    return high, coords - 4.0 * high
 
 
 def three_parts(value):
@@ -43,7 +51,7 @@
     dests = row_ref.shape[0] // 2
     weight = weight_ref[...]
     ones, blank = jnp.ones((1, width), jnp.float32), jnp.zeros((8, width), jnp.float32)
-    total = sum(row_ref[k, 0:8, :].astype(jnp.float32) for k in range(2 * dests))
+    total = sum(halves_of(row_ref[k])[0] for k in range(2 * dests))
     centre = jnp.round(jnp.sum(total, axis=1, keepdims=True) * (1.0 / (2 * dests * width)))
     low = jnp.concatenate([col_ref[piece, 0:modes, :] for piece in range(pieces)], axis=1)
     for piece in range(pieces):
@@ -55,8 +63,8 @@
     for which, half in enumerate(halves):
         core = core_ref[0] if half == 0 else 1 - core_ref[0]
         for y in range(dests):
-            high, rest = split(row_ref[2 * y + core], centre)
-            place = high + rest
+            high, rest = halves_of(row_ref[2 * y + core])
+            place = (high - centre) * 4.0 + rest
             norm = jnp.sum(weight * place * place, axis=0, keepdims=True) + LOG2E * LOG2E
             norms = jnp.concatenate(three_parts(norm) + [ones] * 3 + [blank[0:2]], axis=0)
             cross = three_parts(-2.0 * weight * place)
@@ -107,19 +115,11 @@
     )
 
 
-def row_kernel(coord_ref, out_ref):
-    coords = coord_ref[...].astype(jnp.float32)
-    high = jnp.floor(coords * 0.25)
-    blank = jnp.zeros((5, coords.shape[1]), jnp.float32)
-    pack = jnp.concatenate([high, blank, coords - 4.0 * high, blank], axis=0).astype(jnp.bfloat16)
-    for k in range(out_ref.shape[0]):
-        out_ref[k] = pack
-
-
-def block_kernel(range_ref, row_ref, mode_ref, out_ref, weight_ref):
+def block_kernel(range_ref, coord_ref, mode_ref, out_ref, weight_ref):
     scale = scale_rows(range_ref)
     weight_ref[...] = scale * scale
-    pack = jnp.concatenate([mode_ref[...].astype(jnp.bfloat16), row_ref[0]], axis=0)
+    coords = jnp.concatenate(halves_of(coord_ref[...]), axis=0).astype(jnp.bfloat16)
+    pack = jnp.concatenate([mode_ref[...].astype(jnp.bfloat16), coords], axis=0)
     for k in range(out_ref.shape[0]):
         out_ref[k] = pack
 
@@ -270,11 +270,12 @@
 
 def body(node_coords, inv_range, mode_block):
     modes, width = mode_block.shape
-    near_axes, far_axes, last = ("xl", "zl", "yl"), ("zh", "yh"), "xh"
+    near_axes, far_axes, last = ("xh", "zl", "yl"), ("zh", "yh"), "xl"
     count = {axis: lax.axis_size(axis) for axis in near_axes + far_axes + (last, "c")}
     dests, sources = (math.prod(count[axis] for axis in axes) for axes in (near_axes, far_axes))
     node_total = math.prod(count.values()) * width
-    row_send = call(row_kernel, jax.ShapeDtypeStruct((2 * dests, 16, width), jnp.bfloat16), node_coords)
+    row_send = jnp.pad(node_coords, ((0, 8 - node_coords.shape[0]), (0, 0)))
+    row_send = jnp.broadcast_to(row_send[None], (2 * dests,) + row_send.shape)
     row_pack = lax.all_to_all(row_send, near_axes + ("c",), 0, 0)
     vmem = pl.BlockSpec(memory_space=pltpu.VMEM)
     block, weight = pl.pallas_call(
@@ -285,7 +286,7 @@
         ),
         in_specs=[pl.BlockSpec(memory_space=pltpu.SMEM), vmem, vmem],
         compiler_params=PARAMS,
-    )(inv_range, row_send, mode_block)
+    )(inv_range, node_coords, mode_block)
     block, row_pack = lax.optimization_barrier((block, row_pack))
     block = lax.all_to_all(block, far_axes, 0, 0)
     other = lax.ppermute(block, last, [(0, 1), (1, 0)])
@@ -296,8 +297,8 @@
     far = lax.ppermute(far, "c", [(0, 1), (1, 0)])
     (near,) = shared(other, (0,), (near,))
     pieces = lax.all_to_all(near + far, near_axes, 0, 0)
-    split_axes = (last,) + near_axes + ("c",)
-    slots = math.prod(count[axis] for axis in split_axes)
+    split_axes, joint_axes = (last,) + near_axes + ("c",), far_axes
+    slots, joined = (math.prod(count[axis] for axis in axes) for axes in (split_axes, joint_axes))
     levels = -(-2 * (modes // 8) // slots)
     image, grams = call(
         gram_kernel,
@@ -308,7 +309,7 @@
         pieces,
         mode_block,
     )
-    for axes, copies in ((split_axes, sources), (far_axes, slots)):
+    for axes, copies in ((split_axes, joined), (joint_axes, slots)):
         grams = lax.all_to_all(grams, axes, 0, 0)
         grams = call(spread_kernel, jax.ShapeDtypeStruct((copies, 8 * levels, width), jnp.float32), grams)
     grams = lax.all_to_all(grams, split_axes, 0, 0)

time: 130 us -> 132 us (1.015)
  waiting for transfers between devices: 6.51 us -> 8.92 us
  starting transfers between devices: 20.1 us -> 17.9 us
  blocking collectives: 80 us -> 81.8 us
    ppermute x1, starting transfers between devices: 4.35 us -> 2.21 us  [body(): other = lax.ppermute(block, last, [(0, 1), (1, 0)])]
    all_to_all x1, waiting for transfers between devices: 4.22 us -> 6.04 us  [body(): row_pack = lax.all_to_all(row_send, near_axes + ('c',), 0, 0)]
    all_to_all x1, blocking collectives: 27.1 us -> 28.7 us  [body(): block = lax.all_to_all(block, far_axes, 0, 0)]
    all_to_all x1, blocking collectives: 10.9 us -> 12.4 us  [body(): pieces = lax.all_to_all(near + far, near_axes, 0, 0)]
    pallas_call x5 -> x4, Pallas kernels: 7.36 us -> 6.73 us  [call(): pl.pallas_call(kernel, out_shape=out_shape, compiler_params=PARAMS)(*args)]
where the time goes in v7:
time: 132 us; the launch traced here: 131 us
  blocking collectives  81.8 us (62%)
  Pallas kernels  20.5 us (16%)
  starting transfers between devices  17.9 us (14%)
  waiting for transfers between devices  8.92 us (7%)
  local copies, waits for them, and re-layouts  1.32 us (1%)
    all_to_all x2, blocking collectives, body(): grams = lax.all_to_all(grams, axes, 0, 0)  28.9 us
    all_to_all x1, blocking collectives, body(): block = lax.all_to_all(block, far_axes, 0, 0)  28.7 us
    pallas_call x3, Pallas kernels, covariance_part(): pl.pallas_call(functools.partial(cov_kernel, halves, modes), out_shape=[j...  13.2 us
    all_to_all x1, blocking collectives, body(): pieces = lax.all_to_all(near + far, near_axes, 0, 0)  12.4 us
    all_to_all x1, blocking collectives, body(): grams = lax.all_to_all(grams, split_axes, 0, 0)  11.8 us
    all_to_all x1, starting transfers between devices, body(): row_pack = lax.all_to_all(row_send, near_axes + ('c',), 0, 0)  10.3 us
    pallas_call x4, Pallas kernels, call(): pl.pallas_call(kernel, out_shape=out_shape, compiler_params=PARAMS)(*args)  6.73 us
    all_to_all x1, waiting for transfers between devices, body(): row_pack = lax.all_to_all(row_send, near_axes + ('c',), 0, 0)  6.04 us
  transfers between devices with their start and end apart: 3, of which 2 were waited for; matrix products, arithmetic and copies ran while one was open for 0% of the time, Pallas kernels for 8%

profile of v7, /device:TPU:1, one launch (start us, length us, event | category | flops | bytes accessed | tf_op | source)
XLA Modules:
  0.0 131.3 jit_solution(11166763465960418275)
XLA Ops:
  0.6 0.7 pad.4
  1.3 0.6 broadcast_in_dim.10
  1.9 0.0 copy-start
  1.9 0.0 copy-start.1
  1.9 0.0 copy-start.2
  1.9 10.3 %all-to-all-start = ((s32[16,8,128]{2,1,0:T(8,128)}), s32[16,8,128]{2,1,0:T(8,128)S(1)}, u32[]{:S(2)}, u32[]{:S(2)}) async-start(s32[16,8,128]{2,1,0:T(8,128)} %broadcast_in_dim.10), calls=%async_computation | async-start | bytes 131072 | tf_op jit(solution)/shard_map/all_to_all | solution.py:279
  12.2 0.0 copy-done
  12.2 0.0 copy-done.1
  12.2 0.0 copy-done.2
  12.3 0.6 shard_map.50
  12.8 6.0 %all-to-all-done.row_ref = s32[16,8,128]{2,1,0:T(8,128)S(1)} async-done(((s32[16,8,128]{2,1,0:T(8,128)}), s32[16,8,128]{2,1,0:T(8,128)S(1)}, u32[]{:S(2)}, u32[]{:S(2)}) %all-to-all-start) | async-done | bytes 65568 | tf_op jit(solution)/shard_map/all_to_all | solution.py:279
  18.9 28.7 %all_to_all.30.col_ref = bf16[16,112,128]{2,1,0:T(8,128)(2,1)S(1)} all-to-all(bf16[16,112,128]{2,1,0:T(8,128)(2,1)S(1)} %get-tuple-element.13), channel_id=1, replica_groups=mesh['xh'=2,'xl'=2,'zh'=4,'zl'=2,'yh'=4,'yl'=2,'c'=2] {'zh','yh'}, dimensions={0} | all-to-all | bytes 917504 | tf_op jit(solution)/shard_map/all_to_all | solution.py:291
  47.6 2.2 %collective-permute-start = (bf16[16,112,128]{2,1,0:T(8,128)(2,1)S(1)}, bf16[16,112,128]{2,1,0:T(8,128)(2,1)S(1)}, u32[]{:S(2)}, u32[]{:S(2)}) collective-permute-start(bf16[16,112,128]{2,1,0:T(8,128)(2,1)S(1)} %all_to_all.30.col_ref), channel_id=1, source_target_pairs={{0,128},{128,0},{1,129},{129,1},{2,130},{130,2},{3,131},{131,3},{4... | collective-permute-start | bytes 1376264 | tf_op jit(solution)/shard_map/ppermute | solution.py:292
  49.8 6.4 %shard_map.51 = (f32[8,96,128]{2,1,0:T(8,128)S(1)}, f32[8,96,128]{2,1,0:T(8,128)S(1)}) custom-call(s32[1]{0:T(128)} %bitcast.core_ref, f32[8,128]{1,0:T(8,128)S(1)} %get-tuple-element.10.weight_ref, s32[16,8,128]{2,1,0:T(8,128)S(1)} %all-to-all-done.row_ref, bf16[16,112,128]{2,1,0:T(8,128)(2,1)S(1)} %all_to_all.30.col_ref), custom_call_target="tpu_custom_call" | custom-call | flops 3221225472 | bytes 393216 | tf_op jit(solution)/shard_map/pallas_call | solution.py:95
  56.1 2.9 %collective-permute-done.col_ref = bf16[16,112,128]{2,1,0:T(8,128)(2,1)S(1)} collective-permute-done((bf16[16,112,128]{2,1,0:T(8,128)(2,1)S(1)}, bf16[16,112,128]{2,1,0:T(8,128)(2,1)S(1)}, u32[]{:S(2)}, u32[]{:S(2)}) %collective-permute-start) | collective-permute-done | bytes 458784 | tf_op jit(solution)/shard_map/ppermute | solution.py:292
  59.0 3.4 %shard_map.53 = f32[8,96,128]{2,1,0:T(8,128)S(1)} custom-call(s32[1]{0:T(128)} %bitcast.core_ref, f32[8,128]{1,0:T(8,128)S(1)} %get-tuple-element.10.weight_ref, s32[16,8,128]{2,1,0:T(8,128)S(1)} %all-to-all-done.row_ref, bf16[16,112,128]{2,1,0:T(8,128)(2,1)S(1)} %collective-permute-done.col_ref, ...), custom_call_target="tpu_custom_call", output_to_operand_aliasing={{}: (4, {})} | custom-call | flops 1610612736 | bytes 393216 | tf_op jit(solution)/shard_map/pallas_call | solution.py:95
  62.5 5.4 %collective-permute-start.1 = (f32[8,96,128]{2,1,0:T(8,128)S(1)}, f32[8,96,128]{2,1,0:T(8,128)S(1)}, u32[]{:S(2)}, u32[]{:S(2)}) collective-permute-start(f32[8,96,128]{2,1,0:T(8,128)S(1)} %shard_map.53), channel_id=1, source_target_pairs={{0,1},{1,0},{2,3},{3,2},{4,5},{5,4},{6,7},{7,6},{8,9},{9,8},{10,11... | collective-permute-start | bytes 1179656 | tf_op jit(solution)/shard_map/ppermute | solution.py:297
  67.9 3.4 %shard_map.52 = f32[8,96,128]{2,1,0:T(8,128)S(1)} custom-call(s32[1]{0:T(128)} %bitcast.core_ref, f32[8,128]{1,0:T(8,128)S(1)} %get-tuple-element.10.weight_ref, s32[16,8,128]{2,1,0:T(8,128)S(1)} %all-to-all-done.row_ref, bf16[16,112,128]{2,1,0:T(8,128)(2,1)S(1)} %collective-permute-done.col_ref, ...), custom_call_target="tpu_custom_call", output_to_operand_aliasing={{}: (4, {})} | custom-call | flops 1610612736 | bytes 393216 | tf_op jit(solution)/shard_map/pallas_call | solution.py:95
  71.3 0.0 collective-permute-done.1
  71.4 12.4 %all_to_all.31.part_ref = f32[8,96,128]{2,1,0:T(8,128)S(1)} all-to-all(f32[8,96,128]{2,1,0:T(8,128)S(1)} %add.5), channel_id=1, replica_groups=mesh['xh'=2,'xl'=2,'zh'=4,'zl'=2,'yh'=4,'yl'=2,'c'=2] {'xh','zl','yl'}, dimensions={0} | all-to-all | bytes 786432 | tf_op jit(solution)/shard_map/all_to_all | solution.py:299
  83.8 0.5 shard_map.54
  84.4 11.1 %all_to_all.32.part_ref = f32[32,8,128]{2,1,0:T(8,128)S(1)} all-to-all(f32[32,8,128]{2,1,0:T(8,128)S(1)} %get-tuple-element.16), channel_id=1, replica_groups=mesh['xh'=2,'xl'=2,'zh'=4,'zl'=2,'yh'=4,'yl'=2,'c'=2] {'xl','xh','zl','y..., dimensions={0} | all-to-all | bytes 262144 | tf_op jit(solution)/shard_map/all_to_all | solution.py:313
  95.5 17.8 %all_to_all.33.part_ref = f32[16,8,128]{2,1,0:T(8,128)S(1)} all-to-all(f32[16,8,128]{2,1,0:T(8,128)S(1)} %shard_map.55), channel_id=1, replica_groups=mesh['xh'=2,'xl'=2,'zh'=4,'zl'=2,'yh'=4,'yl'=2,'c'=2] {'zh','yh'}, dimensions={0} | all-to-all | bytes 131072 | tf_op jit(solution)/shard_map/all_to_all | solution.py:313
  113.3 11.8 %all_to_all.34.gram_ref = f32[32,8,128]{2,1,0:T(8,128)S(1)} all-to-all(f32[32,8,128]{2,1,0:T(8,128)S(1)} %shard_map.56), channel_id=1, replica_groups=mesh['xh'=2,'xl'=2,'zh'=4,'zl'=2,'yh'=4,'yl'=2,'c'=2] {'xl','xh','zl','y..., dimensions={0} | all-to-all | bytes 262144 | tf_op jit(solution)/shard_map/all_to_all | solution.py:315
  125.1 6.2 %shard_map.57 = (f32[96,128]{1,0:T(8,128)}, f32[96,96]{1,0:T(8,128)}) custom-call(f32[32,8,128]{2,1,0:T(8,128)S(1)} %all_to_all.34.gram_ref, f32[96,128]{1,0:T(8,128)S(1)} %get-tuple-element.17.image_ref), custom_call_target="tpu_custom_call" | custom-call | tf_op jit(solution)/shard_map/pallas_call | solution.py:268
  (3 shorter events, 0.1 us)
Async XLA Ops:
  1.9 10.3 %copy-start = (f32[96,128]{1,0:T(8,128)S(1)}, f32[96,128]{1,0:T(8,128)}, u32[]{:S(2)}) copy-start(f32[96,128]{1,0:T(8,128)} %mode_ref.3) | copy-start | bytes 147460
  1.9 10.3 %copy-start.1 = (s32[3,128]{1,0:T(4,128)S(1)}, s32[3,128]{1,0:T(4,128)}, u32[]{:S(2)}) copy-start(s32[3,128]{1,0:T(4,128)} %coord_ref.1) | copy-start | bytes 4612
  1.9 10.3 %copy-start.2 = (f32[3]{0:T(128)S(1)}, f32[3]{0:T(128)}, u32[]{:S(2)}) copy-start(f32[3]{0:T(128)} %range_ref.1) | copy-start | bytes 40
  1.9 16.9 %all-to-all-start = ((s32[16,8,128]{2,1,0:T(8,128)}), s32[16,8,128]{2,1,0:T(8,128)S(1)}, u32[]{:S(2)}, u32[]{:S(2)}) async-start(s32[16,8,128]{2,1,0:T(8,128)} %broadcast_in_dim.10), calls=%async_computation | async-start | bytes 131072 | tf_op jit(solution)/shard_map/all_to_all | solution.py:279
  47.6 11.5 %collective-permute-start = (bf16[16,112,128]{2,1,0:T(8,128)(2,1)S(1)}, bf16[16,112,128]{2,1,0:T(8,128)(2,1)S(1)}, u32[]{:S(2)}, u32[]{:S(2)}) collective-permute-start(bf16[16,112,128]{2,1,0:T(8,128)(2,1)S(1)} %all_to_all.30.col_ref), channel_id=1, source_target_pairs={{0,128},{128,0},{1,129},{129,1},{2,130},{130,2},{3,131},{131,3},{4... | collective-permute-start | bytes 1376264 | tf_op jit(solution)/shard_map/ppermute | solution.py:292
  62.5 8.9 %collective-permute-start.1 = (f32[8,96,128]{2,1,0:T(8,128)S(1)}, f32[8,96,128]{2,1,0:T(8,128)S(1)}, u32[]{:S(2)}, u32[]{:S(2)}) collective-permute-start(f32[8,96,128]{2,1,0:T(8,128)S(1)} %shard_map.53), channel_id=1, source_target_pairs={{0,1},{1,0},{2,3},{3,2},{4,5},{5,4},{6,7},{7,6},{8,9},{9,8},{10,11... | collective-permute-start | bytes 1179656 | tf_op jit(solution)/shard_map/ppermute | solution.py:297

commit v8 on v7

--- a/solution.py
+++ b/solution.py
@@ -31,8 +31,7 @@
 
 def halves_of(coords):
     coords = coords.astype(jnp.float32)
-    if coords.shape[0] < 8:
-        coords = jnp.concatenate([coords, jnp.zeros((8 - coords.shape[0], coords.shape[1]), jnp.float32)], axis=0)
+    coords = jnp.concatenate([coords, jnp.zeros((8 - coords.shape[0], coords.shape[1]), jnp.float32)], axis=0)
     high = jnp.floor(coords * 0.25)
     return high, coords - 4.0 * high
 
@@ -70,7 +69,7 @@
             cross = three_parts(-2.0 * weight * place)
             features = jnp.concatenate(cross + cross + [norms, blank], axis=0)
             rows[which, :, y * width : (y + 1) * width] = features.astype(jnp.bfloat16)
-        group = 4
+        group = dests
         for first in range(0, dests, group):
             span = slice(first * width, (first + group) * width)
             total = jnp.dot(cols[...], rows[which, :, span], preferred_element_type=jnp.float32)
@@ -270,12 +269,11 @@
 
 def body(node_coords, inv_range, mode_block):
     modes, width = mode_block.shape
-    near_axes, far_axes, last = ("xh", "zl", "yl"), ("zh", "yh"), "xl"
+    near_axes, far_axes, last = ("xl", "zl", "yl"), ("zh", "yh"), "xh"
     count = {axis: lax.axis_size(axis) for axis in near_axes + far_axes + (last, "c")}
     dests, sources = (math.prod(count[axis] for axis in axes) for axes in (near_axes, far_axes))
     node_total = math.prod(count.values()) * width
-    row_send = jnp.pad(node_coords, ((0, 8 - node_coords.shape[0]), (0, 0)))
-    row_send = jnp.broadcast_to(row_send[None], (2 * dests,) + row_send.shape)
+    row_send = jnp.broadcast_to(node_coords[None], (2 * dests,) + node_coords.shape)
     row_pack = lax.all_to_all(row_send, near_axes + ("c",), 0, 0)
     vmem = pl.BlockSpec(memory_space=pltpu.VMEM)
     block, weight = pl.pallas_call(

time: 132 us -> 129 us (0.977)
  starting transfers between devices: 17.9 us -> 20.2 us
  blocking collectives: 81.8 us -> 79.7 us
  waiting for transfers between devices: 8.92 us -> 6.95 us
    ppermute x1, starting transfers between devices: 2.21 us -> 4.35 us  [body(): other = lax.ppermute(block, last, [(0, 1), (1, 0)])]
    all_to_all x1, blocking collectives: 12.4 us -> 10.6 us  [body(): pieces = lax.all_to_all(near + far, near_axes, 0, 0)]
    all_to_all x1, blocking collectives: 28.7 us -> 27 us  [body(): block = lax.all_to_all(block, far_axes, 0, 0)]
    all_to_all x1, waiting for transfers between devices: 6.04 us -> 4.44 us  [body(): row_pack = lax.all_to_all(row_send, near_axes + ('c',), 0, 0)]
    all_to_all x2, blocking collectives: 28.9 us -> 30.3 us  [body(): grams = lax.all_to_all(grams, axes, 0, 0)]
where the time goes in v8:
time: 129 us
  blocking collectives  79.7 us (62%)
  starting transfers between devices  20.2 us (16%)
  Pallas kernels  19.7 us (15%)
  waiting for transfers between devices  6.95 us (5%)
  local copies, waits for them, and re-layouts  1.32 us (1%)
    all_to_all x2, blocking collectives, body(): grams = lax.all_to_all(grams, axes, 0, 0)  30.3 us
    all_to_all x1, blocking collectives, body(): block = lax.all_to_all(block, far_axes, 0, 0)  27 us
    pallas_call x3, Pallas kernels, covariance_part(): pl.pallas_call(functools.partial(cov_kernel, halves, modes), out_shape=[j...  12.4 us
    all_to_all x1, blocking collectives, body(): grams = lax.all_to_all(grams, split_axes, 0, 0)  11.7 us
    all_to_all x1, blocking collectives, body(): pieces = lax.all_to_all(near + far, near_axes, 0, 0)  10.6 us
    all_to_all x1, starting transfers between devices, body(): row_pack = lax.all_to_all(row_send, near_axes + ('c',), 0, 0)  10.3 us
    pallas_call x4, Pallas kernels, call(): pl.pallas_call(kernel, out_shape=out_shape, compiler_params=PARAMS)(*args)  6.73 us
    ppermute x1, starting transfers between devices, body(): far = lax.ppermute(far, 'c', [(0, 1), (1, 0)])  5.58 us
  transfers between devices with their start and end apart: 3, of which 2 were waited for; matrix products, arithmetic and copies ran while one was open for 0% of the time, Pallas kernels for 8%

profile of v8, /device:TPU:1, one launch (start us, length us, event | category | flops | bytes accessed | tf_op | source)
XLA Modules:
  0.0 128.6 jit_solution(15991425270274326608)
XLA Ops:
  0.6 0.0 copy-start
  0.6 1.3 %broadcast_in_dim.10 = s32[16,3,128]{2,1,0:T(4,128)} broadcast(s32[3,128]{1,0:T(4,128)} %coord_ref.1), dimensions={1,2} | broadcast | bytes 26112 | tf_op jit(solution)/shard_map/broadcast_in_dim | solution.py:276
  2.0 0.0 copy-start.1
  2.0 0.0 copy-start.2
  2.0 10.3 %all-to-all-start = ((s32[16,3,128]{2,1,0:T(4,128)}), s32[16,3,128]{2,1,0:T(4,128)S(1)}, u32[]{:S(2)}, u32[]{:S(2)}) async-start(s32[16,3,128]{2,1,0:T(4,128)} %broadcast_in_dim.10), calls=%async_computation | async-start | bytes 65536 | tf_op jit(solution)/shard_map/all_to_all | solution.py:277
  12.3 0.0 copy-done
  12.3 0.0 copy-done.1
  12.3 0.0 copy-done.2
  12.3 0.6 shard_map.50
  12.9 4.4 %all-to-all-done.row_ref = s32[16,3,128]{2,1,0:T(4,128)S(1)} async-done(((s32[16,3,128]{2,1,0:T(4,128)}), s32[16,3,128]{2,1,0:T(4,128)S(1)}, u32[]{:S(2)}, u32[]{:S(2)}) %all-to-all-start) | async-done | bytes 24608 | tf_op jit(solution)/shard_map/all_to_all | solution.py:277
  17.3 27.0 %all_to_all.30.col_ref = bf16[16,112,128]{2,1,0:T(8,128)(2,1)S(1)} all-to-all(bf16[16,112,128]{2,1,0:T(8,128)(2,1)S(1)} %get-tuple-element.13), channel_id=1, replica_groups=mesh['xh'=2,'xl'=2,'zh'=4,'zl'=2,'yh'=4,'yl'=2,'c'=2] {'zh','yh'}, dimensions={0} | all-to-all | bytes 917504 | tf_op jit(solution)/shard_map/all_to_all | solution.py:289
  44.3 4.3 %collective-permute-start = (bf16[16,112,128]{2,1,0:T(8,128)(2,1)S(1)}, bf16[16,112,128]{2,1,0:T(8,128)(2,1)S(1)}, u32[]{:S(2)}, u32[]{:S(2)}) collective-permute-start(bf16[16,112,128]{2,1,0:T(8,128)(2,1)S(1)} %all_to_all.30.col_ref), channel_id=1, source_target_pairs={{0,256},{256,0},{1,257},{257,1},{2,258},{258,2},{3,259},{259,3},{4... | collective-permute-start | bytes 1376264 | tf_op jit(solution)/shard_map/ppermute | solution.py:290
  48.7 6.0 %shard_map.51 = (f32[8,96,128]{2,1,0:T(8,128)S(1)}, f32[8,96,128]{2,1,0:T(8,128)S(1)}) custom-call(s32[1]{0:T(128)} %bitcast.core_ref, f32[8,128]{1,0:T(8,128)S(1)} %get-tuple-element.10.weight_ref, s32[16,3,128]{2,1,0:T(4,128)S(1)} %all-to-all-done.row_ref, bf16[16,112,128]{2,1,0:T(8,128)(2,1)S(1)} %all_to_all.30.col_ref), custom_call_target="tpu_custom_call" | custom-call | flops 3221225472 | bytes 393216 | tf_op jit(solution)/shard_map/pallas_call | solution.py:94
  54.7 2.5 %collective-permute-done.col_ref = bf16[16,112,128]{2,1,0:T(8,128)(2,1)S(1)} collective-permute-done((bf16[16,112,128]{2,1,0:T(8,128)(2,1)S(1)}, bf16[16,112,128]{2,1,0:T(8,128)(2,1)S(1)}, u32[]{:S(2)}, u32[]{:S(2)}) %collective-permute-start) | collective-permute-done | bytes 458784 | tf_op jit(solution)/shard_map/ppermute | solution.py:290
  57.2 3.2 %shard_map.53 = f32[8,96,128]{2,1,0:T(8,128)S(1)} custom-call(s32[1]{0:T(128)} %bitcast.core_ref, f32[8,128]{1,0:T(8,128)S(1)} %get-tuple-element.10.weight_ref, s32[16,3,128]{2,1,0:T(4,128)S(1)} %all-to-all-done.row_ref, bf16[16,112,128]{2,1,0:T(8,128)(2,1)S(1)} %collective-permute-done.col_ref, ...), custom_call_target="tpu_custom_call", output_to_operand_aliasing={{}: (4, {})} | custom-call | flops 1610612736 | bytes 393216 | tf_op jit(solution)/shard_map/pallas_call | solution.py:94
  60.4 5.6 %collective-permute-start.1 = (f32[8,96,128]{2,1,0:T(8,128)S(1)}, f32[8,96,128]{2,1,0:T(8,128)S(1)}, u32[]{:S(2)}, u32[]{:S(2)}) collective-permute-start(f32[8,96,128]{2,1,0:T(8,128)S(1)} %shard_map.53), channel_id=1, source_target_pairs={{0,1},{1,0},{2,3},{3,2},{4,5},{5,4},{6,7},{7,6},{8,9},{9,8},{10,11... | collective-permute-start | bytes 1179656 | tf_op jit(solution)/shard_map/ppermute | solution.py:295
  66.0 3.2 %shard_map.52 = f32[8,96,128]{2,1,0:T(8,128)S(1)} custom-call(s32[1]{0:T(128)} %bitcast.core_ref, f32[8,128]{1,0:T(8,128)S(1)} %get-tuple-element.10.weight_ref, s32[16,3,128]{2,1,0:T(4,128)S(1)} %all-to-all-done.row_ref, bf16[16,112,128]{2,1,0:T(8,128)(2,1)S(1)} %collective-permute-done.col_ref, ...), custom_call_target="tpu_custom_call", output_to_operand_aliasing={{}: (4, {})} | custom-call | flops 1610612736 | bytes 393216 | tf_op jit(solution)/shard_map/pallas_call | solution.py:94
  69.2 0.0 collective-permute-done.1
  69.3 10.6 %all_to_all.31.part_ref = f32[8,96,128]{2,1,0:T(8,128)S(1)} all-to-all(f32[8,96,128]{2,1,0:T(8,128)S(1)} %add.3), channel_id=1, replica_groups=mesh['xh'=2,'xl'=2,'zh'=4,'zl'=2,'yh'=4,'yl'=2,'c'=2] {'xl','zl','yl'}, dimensions={0} | all-to-all | bytes 786432 | tf_op jit(solution)/shard_map/all_to_all | solution.py:297
  79.8 0.5 shard_map.54
  80.3 12.3 %all_to_all.32.part_ref = f32[32,8,128]{2,1,0:T(8,128)S(1)} all-to-all(f32[32,8,128]{2,1,0:T(8,128)S(1)} %get-tuple-element.16), channel_id=1, replica_groups=mesh['xh'=2,'xl'=2,'zh'=4,'zl'=2,'yh'=4,'yl'=2,'c'=2] {'xh','xl','zl','y..., dimensions={0} | all-to-all | bytes 262144 | tf_op jit(solution)/shard_map/all_to_all | solution.py:311
  92.7 18.0 %all_to_all.33.part_ref = f32[16,8,128]{2,1,0:T(8,128)S(1)} all-to-all(f32[16,8,128]{2,1,0:T(8,128)S(1)} %shard_map.55), channel_id=1, replica_groups=mesh['xh'=2,'xl'=2,'zh'=4,'zl'=2,'yh'=4,'yl'=2,'c'=2] {'zh','yh'}, dimensions={0} | all-to-all | bytes 131072 | tf_op jit(solution)/shard_map/all_to_all | solution.py:311
  110.7 11.7 %all_to_all.34.gram_ref = f32[32,8,128]{2,1,0:T(8,128)S(1)} all-to-all(f32[32,8,128]{2,1,0:T(8,128)S(1)} %shard_map.56), channel_id=1, replica_groups=mesh['xh'=2,'xl'=2,'zh'=4,'zl'=2,'yh'=4,'yl'=2,'c'=2] {'xh','xl','zl','y..., dimensions={0} | all-to-all | bytes 262144 | tf_op jit(solution)/shard_map/all_to_all | solution.py:313
  122.5 6.2 %shard_map.57 = (f32[96,128]{1,0:T(8,128)}, f32[96,96]{1,0:T(8,128)}) custom-call(f32[32,8,128]{2,1,0:T(8,128)S(1)} %all_to_all.34.gram_ref, f32[96,128]{1,0:T(8,128)S(1)} %get-tuple-element.17.image_ref), custom_call_target="tpu_custom_call" | custom-call | tf_op jit(solution)/shard_map/pallas_call | solution.py:267
  (3 shorter events, 0.1 us)
Async XLA Ops:
  0.6 11.6 %copy-start = (f32[96,128]{1,0:T(8,128)S(1)}, f32[96,128]{1,0:T(8,128)}, u32[]{:S(2)}) copy-start(f32[96,128]{1,0:T(8,128)} %mode_ref.3) | copy-start | bytes 147460
  2.0 10.3 %copy-start.1 = (s32[3,128]{1,0:T(4,128)S(1)}, s32[3,128]{1,0:T(4,128)}, u32[]{:S(2)}) copy-start(s32[3,128]{1,0:T(4,128)} %coord_ref.1) | copy-start | bytes 4612
  2.0 10.3 %copy-start.2 = (f32[3]{0:T(128)S(1)}, f32[3]{0:T(128)}, u32[]{:S(2)}) copy-start(f32[3]{0:T(128)} %range_ref.1) | copy-start | bytes 40
  2.0 15.3 %all-to-all-start = ((s32[16,3,128]{2,1,0:T(4,128)}), s32[16,3,128]{2,1,0:T(4,128)S(1)}, u32[]{:S(2)}, u32[]{:S(2)}) async-start(s32[16,3,128]{2,1,0:T(4,128)} %broadcast_in_dim.10), calls=%async_computation | async-start | bytes 65536 | tf_op jit(solution)/shard_map/all_to_all | solution.py:277
  44.3 12.8 %collective-permute-start = (bf16[16,112,128]{2,1,0:T(8,128)(2,1)S(1)}, bf16[16,112,128]{2,1,0:T(8,128)(2,1)S(1)}, u32[]{:S(2)}, u32[]{:S(2)}) collective-permute-start(bf16[16,112,128]{2,1,0:T(8,128)(2,1)S(1)} %all_to_all.30.col_ref), channel_id=1, source_target_pairs={{0,256},{256,0},{1,257},{257,1},{2,258},{258,2},{3,259},{259,3},{4... | collective-permute-start | bytes 1376264 | tf_op jit(solution)/shard_map/ppermute | solution.py:290
  60.4 8.8 %collective-permute-start.1 = (f32[8,96,128]{2,1,0:T(8,128)S(1)}, f32[8,96,128]{2,1,0:T(8,128)S(1)}, u32[]{:S(2)}, u32[]{:S(2)}) collective-permute-start(f32[8,96,128]{2,1,0:T(8,128)S(1)} %shard_map.53), channel_id=1, source_target_pairs={{0,1},{1,0},{2,3},{3,2},{4,5},{5,4},{6,7},{7,6},{8,9},{9,8},{10,11... | collective-permute-start | bytes 1179656 | tf_op jit(solution)/shard_map/ppermute | solution.py:295
